TPU v7x, 128 devices: a whole 4x4x4 slice. The times are simulated.
128 devices in a mesh: ctx: 32 (over z, x_lo, y), ep: 4 (over x_hi, core).
Axes of the slice: x: 4 (x_hi: 2, x_lo: 2; x = x_hi * 2 + x_lo), y: 4, z: 4, core: 2. Of those that a mesh axis runs over, the one named last changes fastest.
Arguments:
- inputs: bfloat16 [2, 8192, 1536], P(None, ('ctx', 'ep')), may hold values from -6 to 6
- cotangent: bfloat16 [2, 8192, 1536], P(None, ('ctx', 'ep')), may hold values from -6 to 6
- segments: int32 [2, 8192], P(None, 'ctx'), may hold values from 0 to 8, as said below
- routes: int32 [2, 8192, 8], P(None, ('ctx', 'ep')), may hold values from 0 to 11, all different within a row; in each aligned block of 64 rows (0 to 63, 64 to 127, ..., all dimensions but the last counted through in order) at most 48 rows name the same one
- attn_gain: bfloat16 [1536], P(('ctx', 'ep')), may hold values from 0.5 to 1.5
- w_query: bfloat16 [1536, 1536], P('ctx', 'ep'), may hold values from -0.15625 to 0.15625
- key_weight: bfloat16 [1536, 512], P('ctx', 'ep'), may hold values from -0.15625 to 0.15625
- value_weight: bfloat16 [1536, 512], P('ctx', 'ep'), may hold values from -0.15625 to 0.15625
- w_out: bfloat16 [1536, 1536], P('ep', 'ctx'), may hold values from -6 to 6
- ffn_gain: bfloat16 [1536], P(('ctx', 'ep')), may hold values from 0.5 to 1.5
- router: bfloat16 [1536, 12], P(('ctx', 'ep')), may hold values from -0.078125 to 0.078125
- w_gate: bfloat16 [12, 1536, 512], P('ep', 'ctx'), may hold values from -0.15625 to 0.15625
- w_up: bfloat16 [12, 1536, 512], P('ep', 'ctx'), may hold values from -0.15625 to 0.15625
- w_down: bfloat16 [12, 512, 1536], P('ep', None, 'ctx'), may hold values from -1 to 1
Outputs:
- outputs: bfloat16 [2, 8192, 1536], P(None, ('ctx', 'ep'))
- input_grad: bfloat16 [2, 8192, 1536], P(None, ('ctx', 'ep'))
- grad_attn_gain: float32 [1536], P(('ctx', 'ep'))
- grad_query: float32 [1536, 1536], P('ctx', 'ep')
- grad_key: float32 [1536, 512], P('ctx', 'ep')
- grad_value: float32 [1536, 512], P('ctx', 'ep')
- grad_out: float32 [1536, 1536], P('ep', 'ctx')
- grad_ffn_gain: float32 [1536], P(('ctx', 'ep'))
- grad_router: float32 [1536, 12], P(('ctx', 'ep'))
- grad_gate: float32 [12, 1536, 512], P('ep', 'ctx')
- grad_up: float32 [12, 1536, 512], P('ep', 'ctx')
- grad_down: float32 [12, 512, 1536], P('ep', None, 'ctx')
Inputs may be any that keep to these rules, and one draw needn't show every extreme that they name: `segments`: never falls along a micro-batch; document 4 starts within the first 256 tokens and ends within the last 256 tokens. `routes`: each token names 8 different experts; within one micro-batch, among the tokens of one device no expert is named more than 48 times.
All inputs are finite; a program needn't handle non-finite values.
Results may differ from a plain program's by a relative error of at most 0.034.
Values may be sent and summed in bfloat16 or wider, within the bound.
No kernel may reach another device: no remote copies, remote signals or barrier semaphores. Data moves between devices by JAX's collectives and lax.ppermute only.
A program may use at most 128 MiB of HBM per device.

v0:
```python
import math

import jax
import jax.numpy as jnp
from jax import lax
from jax.sharding import PartitionSpec as P

HEAD_DIM = 64
EXP_DEV = 3
MB = 2
CAP = 48


EPSILON = 1e-06
MASKED = -1e30


def shifted(value, axis, by):
    size = lax.axis_size(axis)
    pairs = [(i, i + by) for i in range(size) if 0 <= i + by < size]
    return lax.ppermute(value, axis, pairs)


def for_sending(value):

    def short(part):
        return part.astype(jnp.bfloat16) if part.dtype == jnp.float32 else part

    return jax.tree.map(short, value)


def from_behind(block, axis, distance):
    devices = range(lax.axis_size(axis))
    route = [((i - distance) % len(devices), i) for i in devices]
    return lax.ppermute(block, axis, route)


def rms_scale(values):
    return lax.rsqrt(jnp.mean(values * values, axis=-1, keepdims=True) + EPSILON)


def rope_tables(positions, head_width):
    half_width = head_width // 2
    inverse = jnp.exp(
        jnp.arange(half_width, dtype=jnp.float32) * (-2.0 * math.log(10000.0) / head_width)
    )
    angles = positions.astype(jnp.float32)[:, None] * inverse[None, :]
    return (jnp.cos(angles)[:, None, :], jnp.sin(angles)[:, None, :])


def apply_rotation(values, cosine_table, sine_values):
    half_width = values.shape[-1] // 2
    lead_half = values[..., :half_width]
    tail_half = values[..., half_width:]
    return jnp.concatenate(
        [
            lead_half * cosine_table - tail_half * sine_values,
            tail_half * cosine_table + lead_half * sine_values,
        ],
        axis=-1,
    )


def unrotate(grads_in, cosine_table, sine_values):
    half_width = grads_in.shape[-1] // 2
    lead_half = grads_in[..., :half_width]
    tail_half = grads_in[..., half_width:]
    return jnp.concatenate(
        [
            lead_half * cosine_table + tail_half * sine_values,
            tail_half * cosine_table - lead_half * sine_values,
        ],
        axis=-1,
    )


def fetch_weights(local_weights):
    return (
        lax.all_gather(local_weights[0], "ctx", axis=0, tiled=True),
        lax.all_gather(local_weights[1], "ctx", axis=0, tiled=True),
        lax.all_gather(local_weights[2], "ctx", axis=0, tiled=True),
        lax.all_gather(local_weights[3], "ctx", axis=1, tiled=True),
        lax.all_gather(local_weights[4], "ctx", axis=1, tiled=True),
        lax.all_gather(local_weights[5], "ctx", axis=1, tiled=True),
        lax.all_gather(local_weights[6], "ctx", axis=2, tiled=True),
    )


def reduce_grads(weight_grads, small_grads):
    weight_part = (
        lax.psum_scatter(
            weight_grads[0].astype(jnp.bfloat16), "ctx", scatter_dimension=0, tiled=True
        ).astype(jnp.float32),
        lax.psum_scatter(
            weight_grads[1].astype(jnp.bfloat16), "ctx", scatter_dimension=0, tiled=True
        ).astype(jnp.float32),
        lax.psum_scatter(
            weight_grads[2].astype(jnp.bfloat16), "ctx", scatter_dimension=0, tiled=True
        ).astype(jnp.float32),
        lax.psum_scatter(
            weight_grads[3].astype(jnp.bfloat16), "ctx", scatter_dimension=1, tiled=True
        ).astype(jnp.float32),
        lax.psum_scatter(
            weight_grads[4].astype(jnp.bfloat16), "ctx", scatter_dimension=1, tiled=True
        ).astype(jnp.float32),
        lax.psum_scatter(
            weight_grads[5].astype(jnp.bfloat16), "ctx", scatter_dimension=1, tiled=True
        ).astype(jnp.float32),
        lax.psum_scatter(
            weight_grads[6].astype(jnp.bfloat16), "ctx", scatter_dimension=2, tiled=True
        ).astype(jnp.float32),
    )
    small_part = (
        lax.psum_scatter(small_grads[0], ("ctx", "ep"), scatter_dimension=0, tiled=True),
        lax.psum_scatter(small_grads[1], ("ctx", "ep"), scatter_dimension=0, tiled=True),
        lax.psum_scatter(small_grads[2], ("ctx", "ep"), scatter_dimension=0, tiled=True),
    )
    return (weight_part, small_part)


def cycle_pass(step_fn, carry_init, blocks, travel):
    ctx_count = lax.axis_size("ctx")
    my_index = lax.axis_index("ctx")

    def turn(turn_index, loop_state):
        carry_total, held_blocks, moving = loop_state
        source = (my_index - turn_index) % ctx_count
        carry_total, moving = step_fn(carry_total, held_blocks, moving, source)
        held_blocks = shifted((held_blocks[0], held_blocks[1], held_blocks[2]), "ctx", 1)
        if moving is not None:
            moving = jax.tree.map(
                lambda part, own: part.astype(own.dtype),
                from_behind(for_sending(moving), "ctx", 1),
                moving,
            )
        return (carry_total, held_blocks, moving)

    return lax.fori_loop(0, ctx_count, turn, (carry_init, blocks, travel))


def block_scores(query_heads, key_block, query_seg, key_seg, query_pos, key_pos, score_scale):
    scores = (
        jnp.einsum("hgqd,hkd->hgqk", query_heads, key_block, preferred_element_type=jnp.float32)
        * score_scale
    )
    allowed = (query_seg[:, None] == key_seg[None, :]) & (key_pos[None, :] <= query_pos[:, None])
    return jnp.where(allowed, scores, MASKED)


def expert_forward(received, w_gate, w_up, w_down):
    gate_pre = jnp.einsum("erd,edf->erf", received, w_gate, preferred_element_type=jnp.float32)
    up_pre = jnp.einsum("erd,edf->erf", received, w_up, preferred_element_type=jnp.float32)
    hidden = (jax.nn.silu(gate_pre) * up_pre).astype(jnp.bfloat16)
    expert_out = jnp.einsum(
        "erf,efd->erd", hidden, w_down, preferred_element_type=jnp.float32
    ).astype(jnp.bfloat16)
    return (gate_pre, up_pre, hidden, expert_out)


def expert_backward(grad_received, received, gate_pre, up_pre, hidden, w_gate, w_up, w_down):
    grad_hidden = jnp.einsum(
        "erd,efd->erf", grad_received, w_down, preferred_element_type=jnp.float32
    )
    sigmoid_gate = jax.nn.sigmoid(gate_pre)
    grad_gate_pre = (
        grad_hidden * up_pre * sigmoid_gate * (1.0 + gate_pre * (1.0 - sigmoid_gate))
    ).astype(jnp.bfloat16)
    grad_up_pre = (grad_hidden * gate_pre * sigmoid_gate).astype(jnp.bfloat16)
    grad_down = jnp.einsum(
        "erf,erd->efd", hidden, grad_received, preferred_element_type=jnp.float32
    )
    grad_gate = jnp.einsum(
        "erd,erf->edf", received, grad_gate_pre, preferred_element_type=jnp.float32
    )
    grad_up = jnp.einsum("erd,erf->edf", received, grad_up_pre, preferred_element_type=jnp.float32)
    grad_inputs = jnp.einsum(
        "erf,edf->erd", grad_gate_pre, w_gate, preferred_element_type=jnp.float32
    )
    grad_inputs = (
        grad_inputs
        + jnp.einsum("erf,edf->erd", grad_up_pre, w_up, preferred_element_type=jnp.float32)
    ).astype(jnp.bfloat16)
    return (grad_inputs, grad_gate, grad_up, grad_down)


def process(
    input_rows, cotangent_rows, segment_rows, route_rows, small_params, forward_set, backward_set
):
    gain_one = small_params[0].astype(jnp.float32)
    gain_two = small_params[1].astype(jnp.float32)
    router_full = small_params[2]
    w_query, key_weight, value_weight, w_out, w_gate, w_up, w_down = forward_set
    ep_count = lax.axis_size("ep")
    inputs = input_rows.astype(jnp.float32)
    scale_one = rms_scale(inputs)
    normal_one = inputs * scale_one
    normalized_input = (normal_one * gain_one).astype(jnp.bfloat16)
    rows_ctx = lax.all_gather(normalized_input, "ep", axis=0, tiled=True)
    joined = jnp.concatenate([w_query, key_weight, value_weight], axis=1)
    projected = jnp.dot(rows_ctx, joined, preferred_element_type=jnp.float32)
    width_query = w_query.shape[1]
    width_key = key_weight.shape[1]
    heads_query = width_query // HEAD_DIM
    heads_key = width_key // HEAD_DIM
    heads_per_group = heads_query // heads_key
    sequence_length = rows_ctx.shape[0]
    offsets = jnp.arange(sequence_length, dtype=jnp.int32)
    positions = lax.axis_index("ctx") * sequence_length + offsets
    cosine_table, sine_values = rope_tables(positions, HEAD_DIM)
    query_matrix = apply_rotation(
        projected[:, :width_query].reshape(sequence_length, heads_query, HEAD_DIM),
        cosine_table,
        sine_values,
    ).astype(jnp.bfloat16)
    key_matrix = apply_rotation(
        projected[:, width_query : width_query + width_key].reshape(
            sequence_length, heads_key, HEAD_DIM
        ),
        cosine_table,
        sine_values,
    ).astype(jnp.bfloat16)
    value_matrix = (
        projected[:, width_query + width_key :]
        .reshape(sequence_length, heads_key, HEAD_DIM)
        .astype(jnp.bfloat16)
    )
    query_heads = query_matrix.reshape(
        sequence_length, heads_key, heads_per_group, HEAD_DIM
    ).transpose(1, 2, 0, 3)
    blocks = (key_matrix.transpose(1, 0, 2), value_matrix.transpose(1, 0, 2), segment_rows)
    score_scale = 1.0 / math.sqrt(HEAD_DIM)

    def scores_for(held_blocks, source):
        return block_scores(
            query_heads,
            held_blocks[0],
            segment_rows,
            held_blocks[2],
            positions,
            source * sequence_length + offsets,
            score_scale,
        )

    def max_step(carry_total, held_blocks, moving, source):
        row_max, row_total = carry_total
        scores = scores_for(held_blocks, source)
        new_max = jnp.maximum(row_max, jnp.max(scores, axis=-1))
        row_total = row_total * jnp.exp(row_max - new_max) + jnp.sum(
            jnp.exp(scores - new_max[..., None]), axis=-1
        )
        return ((new_max, row_total), moving)

    start_max = jnp.full((heads_key, heads_per_group, sequence_length), MASKED, jnp.float32)
    stats = cycle_pass(max_step, (start_max, jnp.zeros_like(start_max)), blocks, None)[0]
    log_total = stats[0] + jnp.log(stats[1])

    def value_step(carry_total, held_blocks, moving, source):
        weights_p = jnp.exp(scores_for(held_blocks, source) - log_total[..., None]).astype(
            jnp.bfloat16
        )
        return (
            carry_total
            + jnp.einsum(
                "hgqk,hkd->hgqd", weights_p, held_blocks[1], preferred_element_type=jnp.float32
            ),
            moving,
        )

    mixed_heads = cycle_pass(
        value_step,
        jnp.zeros((heads_key, heads_per_group, sequence_length, HEAD_DIM), jnp.float32),
        blocks,
        None,
    )[0]
    mixed = (
        mixed_heads.transpose(2, 0, 1, 3).reshape(sequence_length, width_query).astype(jnp.bfloat16)
    )
    attn_out = lax.psum_scatter(
        jnp.dot(mixed, w_out, preferred_element_type=jnp.float32).astype(jnp.bfloat16),
        "ep",
        scatter_dimension=0,
        tiled=True,
    ).astype(jnp.float32)
    residual = inputs + attn_out
    scale_two = rms_scale(residual)
    normal_two = residual * scale_two
    tokens = (normal_two * gain_two).astype(jnp.bfloat16)
    logits = jnp.dot(tokens, router_full, preferred_element_type=jnp.float32)
    gate_probs = jax.nn.softmax(jnp.take_along_axis(logits, route_rows, axis=1), axis=-1)
    top_count = route_rows.shape[1]
    model_width = tokens.shape[1]
    expert_total = EXP_DEV * ep_count
    expert_ids = jnp.arange(expert_total, dtype=jnp.int32)
    slot_rows = ep_count * CAP
    buffer_rows = EXP_DEV * slot_rows
    grad_out = cotangent_rows.astype(jnp.float32)
    flat_ids = route_rows.reshape(-1)
    onehot = (flat_ids[:, None] == expert_ids[None, :]).astype(jnp.int32)
    slot_rank = jnp.sum((jnp.cumsum(onehot, axis=0) - onehot) * onehot, axis=1)
    slot_dest = (flat_ids % EXP_DEV * ep_count + flat_ids // EXP_DEV) * CAP + slot_rank
    owner_rows = jnp.arange(flat_ids.shape[0], dtype=jnp.int32) // top_count
    send_buffer = (
        jnp.zeros((buffer_rows, model_width), jnp.bfloat16).at[slot_dest].set(tokens[owner_rows])
    )
    received = lax.all_to_all(
        send_buffer.reshape(EXP_DEV, ep_count, CAP, model_width),
        "ep",
        split_axis=1,
        concat_axis=1,
        tiled=True,
    )
    received = received.reshape(EXP_DEV, slot_rows, model_width)
    gate_pre, up_pre, hidden, expert_out = expert_forward(received, w_gate, w_up, w_down)
    returned = lax.all_to_all(
        expert_out.reshape(EXP_DEV, ep_count, CAP, model_width),
        "ep",
        split_axis=1,
        concat_axis=1,
        tiled=True,
    )
    pair_out = (
        returned.reshape(buffer_rows, model_width)[slot_dest]
        .astype(jnp.float32)
        .reshape(-1, top_count, model_width)
    )
    output_rows = (residual + jnp.sum(gate_probs[..., None] * pair_out, axis=1)).astype(
        jnp.bfloat16
    )
    w_query, key_weight, value_weight, w_out, w_gate, w_up, w_down = backward_set
    joined = jnp.concatenate([w_query, key_weight, value_weight], axis=1)
    grad_gates = jnp.sum(grad_out[:, None, :] * pair_out, axis=-1)
    grad_pairs = (gate_probs.reshape(-1)[:, None] * grad_out[owner_rows]).astype(jnp.bfloat16)
    grad_buffer = jnp.zeros((buffer_rows, model_width), jnp.bfloat16).at[slot_dest].set(grad_pairs)
    grad_received = lax.all_to_all(
        grad_buffer.reshape(EXP_DEV, ep_count, CAP, model_width),
        "ep",
        split_axis=1,
        concat_axis=1,
        tiled=True,
    )
    grad_received = grad_received.reshape(EXP_DEV, slot_rows, model_width)
    grad_inputs, grad_gate, grad_up, grad_down = expert_backward(
        grad_received, received, gate_pre, up_pre, hidden, w_gate, w_up, w_down
    )
    grad_back = lax.all_to_all(
        grad_inputs.reshape(EXP_DEV, ep_count, CAP, model_width),
        "ep",
        split_axis=1,
        concat_axis=1,
        tiled=True,
    )
    grad_pair_in = (
        grad_back.reshape(buffer_rows, model_width)[slot_dest]
        .astype(jnp.float32)
        .reshape(-1, top_count, model_width)
    )
    expert_in_grad = jnp.sum(grad_pair_in, axis=1)
    grad_chosen = gate_probs * (
        grad_gates - jnp.sum(gate_probs * grad_gates, axis=-1, keepdims=True)
    )
    choice_table = (route_rows[:, :, None] == expert_ids[None, None, :]).astype(jnp.float32)
    grad_logits = jnp.sum(choice_table * grad_chosen[:, :, None], axis=1).astype(jnp.bfloat16)
    grad_router = jnp.einsum("td,te->de", tokens, grad_logits, preferred_element_type=jnp.float32)
    grad_tokens = jnp.einsum(
        "te,de->td", grad_logits, router_full, preferred_element_type=jnp.float32
    )
    grad_tokens = grad_tokens + expert_in_grad
    grad_gain_two = jnp.sum(grad_tokens * normal_two, axis=0)
    scaled_two = grad_tokens * gain_two
    grad_residual = grad_out + scale_two * (
        scaled_two - normal_two * jnp.mean(scaled_two * normal_two, axis=-1, keepdims=True)
    )
    grad_rows_ctx = lax.all_gather(grad_residual.astype(jnp.bfloat16), "ep", axis=0, tiled=True)
    grad_w_out = jnp.einsum("th,td->hd", mixed, grad_rows_ctx, preferred_element_type=jnp.float32)
    grad_mixed = jnp.einsum(
        "td,hd->th", grad_rows_ctx, w_out, preferred_element_type=jnp.float32
    ).astype(jnp.bfloat16)
    grad_heads = grad_mixed.reshape(
        sequence_length, heads_key, heads_per_group, HEAD_DIM
    ).transpose(1, 2, 0, 3)
    row_delta = jnp.sum(grad_heads.astype(jnp.float32) * mixed_heads, axis=-1)

    def grad_step(carry_total, held_blocks, moving, source):
        weights_p = jnp.exp(scores_for(held_blocks, source) - log_total[..., None])
        grad_keys, grad_values = moving
        grad_values = grad_values + jnp.einsum(
            "hgqk,hgqd->hkd",
            weights_p.astype(jnp.bfloat16),
            grad_heads,
            preferred_element_type=jnp.float32,
        )
        grad_weights = jnp.einsum(
            "hgqd,hkd->hgqk", grad_heads, held_blocks[1], preferred_element_type=jnp.float32
        )
        grad_scores = (weights_p * (grad_weights - row_delta[..., None]) * score_scale).astype(
            jnp.bfloat16
        )
        carry_total = carry_total + jnp.einsum(
            "hgqk,hkd->hgqd", grad_scores, held_blocks[0], preferred_element_type=jnp.float32
        )
        grad_keys = grad_keys + jnp.einsum(
            "hgqk,hgqd->hkd", grad_scores, query_heads, preferred_element_type=jnp.float32
        )
        return (carry_total, (grad_keys, grad_values))

    zero_keys = jnp.zeros((heads_key, sequence_length, HEAD_DIM), jnp.float32)
    final_state = cycle_pass(
        grad_step,
        jnp.zeros((heads_key, heads_per_group, sequence_length, HEAD_DIM), jnp.float32),
        blocks,
        (zero_keys, zero_keys),
    )
    grad_query_heads = final_state[0]
    grad_keys, grad_values = final_state[2]
    grad_query = unrotate(
        grad_query_heads.transpose(2, 0, 1, 3).reshape(sequence_length, heads_query, HEAD_DIM),
        cosine_table,
        sine_values,
    )
    grad_query = grad_query.reshape(sequence_length, width_query).astype(jnp.bfloat16)
    grad_key = (
        unrotate(grad_keys.transpose(1, 0, 2), cosine_table, sine_values)
        .reshape(sequence_length, width_key)
        .astype(jnp.bfloat16)
    )
    grad_value = (
        grad_values.transpose(1, 0, 2).reshape(sequence_length, width_key).astype(jnp.bfloat16)
    )
    grad_joined = jnp.concatenate([grad_query, grad_key, grad_value], axis=1)
    grad_joined_w = jnp.einsum(
        "td,tc->dc", rows_ctx, grad_joined, preferred_element_type=jnp.float32
    )
    grad_partial = jnp.einsum("tc,dc->td", grad_joined, joined, preferred_element_type=jnp.float32)
    grad_normed = lax.psum_scatter(
        grad_partial.astype(jnp.bfloat16), "ep", scatter_dimension=0, tiled=True
    ).astype(jnp.float32)
    grad_gain_one = jnp.sum(grad_normed * normal_one, axis=0)
    scaled_one = grad_normed * gain_one
    grad_input_rows = grad_residual + scale_one * (
        scaled_one - normal_one * jnp.mean(scaled_one * normal_one, axis=-1, keepdims=True)
    )
    weight_grads = (
        grad_joined_w[:, :width_query],
        grad_joined_w[:, width_query : width_query + width_key],
        grad_joined_w[:, width_query + width_key :],
        grad_w_out,
        grad_gate,
        grad_up,
        grad_down,
    )
    return (
        output_rows,
        grad_input_rows.astype(jnp.bfloat16),
        weight_grads,
        (grad_gain_one, grad_gain_two, grad_router),
    )


def local(
    inputs,
    cotangent,
    segments,
    routes,
    attn_gain,
    w_query,
    key_weight,
    value_weight,
    w_out,
    ffn_gain,
    router,
    w_gate,
    w_up,
    w_down,
):
    small_params = (
        lax.all_gather(attn_gain, ("ctx", "ep"), axis=0, tiled=True),
        lax.all_gather(ffn_gain, ("ctx", "ep"), axis=0, tiled=True),
        lax.all_gather(router, ("ctx", "ep"), axis=0, tiled=True),
    )
    local_weights = (w_query, key_weight, value_weight, w_out, w_gate, w_up, w_down)
    output_list = []
    input_grads = []
    weight_sums = None
    small_sums = None
    for micro_batch in range(MB):
        forward_set = fetch_weights(local_weights)
        backward_set = fetch_weights(local_weights)
        output_rows, grad_rows, weight_grads, small_grads = process(
            inputs[micro_batch],
            cotangent[micro_batch],
            segments[micro_batch],
            routes[micro_batch],
            small_params,
            forward_set,
            backward_set,
        )
        output_list.append(output_rows)
        input_grads.append(grad_rows)
        if weight_sums is None:
            weight_sums = weight_grads
            small_sums = small_grads
        else:
            weight_sums = jax.tree.map(jnp.add, weight_sums, weight_grads)
            small_sums = jax.tree.map(jnp.add, small_sums, small_grads)
    weight_sums, small_sums = reduce_grads(weight_sums, small_sums)
    return (
        jnp.stack(output_list),
        jnp.stack(input_grads),
        small_sums[0],
        weight_sums[0],
        weight_sums[1],
        weight_sums[2],
        weight_sums[3],
        small_sums[1],
        small_sums[2],
        weight_sums[4],
        weight_sums[5],
        weight_sums[6],
    )


def solution(mesh):
    placed = (
        P(None, ("ctx", "ep"), None),
        P(None, ("ctx", "ep"), None),
        P(None, "ctx"),
        P(None, ("ctx", "ep"), None),
        P(("ctx", "ep")),
        P("ctx", "ep"),
        P("ctx", "ep"),
        P("ctx", "ep"),
        P("ep", "ctx"),
        P(("ctx", "ep")),
        P(("ctx", "ep"), None),
        P("ep", "ctx", None),
        P("ep", "ctx", None),
        P("ep", None, "ctx"),
    )
    return jax.shard_map(
        local,
        mesh=mesh,
        in_specs=placed,
        out_specs=(
            P(None, ("ctx", "ep"), None),
            P(None, ("ctx", "ep"), None),
            P(("ctx", "ep")),
            P("ctx", "ep"),
            P("ctx", "ep"),
            P("ctx", "ep"),
            P("ep", "ctx"),
            P(("ctx", "ep")),
            P(("ctx", "ep"), None),
            P("ep", "ctx", None),
            P("ep", "ctx", None),
            P("ep", None, "ctx"),
        ),
        check_vma=False,
    )
```

profile of v0, /device:TPU:26, one launch (start us, length us, event | category | flops | bytes accessed | tf_op | source)
XLA Modules:
  0.0 5101.1 jit_solution(6639732290994021045)
XLA Ops:
  12.4 67.3 %all-reduce.7 = (bf16[1536]{0:T(1024)(128)(2,1)S(1)}, bf16[1536]{0:T(1024)(128)(2,1)}) all-reduce(bf16[1536]{0:T(1024)(128)(2,1)S(1)} %dynamic-update-slice, bf16[1536]{0:T(1024)(128)(2,1)S(1)} %dynamic-update-slice.1), channel_id=1, replica_groups=mesh['ctx'=32,'ep'=4] {'ctx','ep'}, use_global_device_ids=true, to_apply=%add | all-reduce | flops 3072 | bytes 12288
  91.9 67.8 %all_gather.31 = bf16[1536,128]{1,0:T(8,128)(2,1)S(1)} all-gather(bf16[48,128]{1,0:T(8,128)(2,1)S(1)} %copy-done.102), channel_id=1, replica_groups=mesh['ctx'=32,'ep'=4] {'ctx'}, dimensions={0}, use_global_device_ids=true | all-gather | bytes 405504 | tf_op jit(solution)/shard_map/all_gather | solution.py:80
  159.7 79.1 %all_gather.32 = bf16[1536,128]{1,0:T(8,128)(2,1)S(1)} all-gather(bf16[48,128]{1,0:T(8,128)(2,1)S(1)} %copy-done.103), channel_id=1, replica_groups=mesh['ctx'=32,'ep'=4] {'ctx'}, dimensions={0}, use_global_device_ids=true | all-gather | bytes 405504 | tf_op jit(solution)/shard_map/all_gather | solution.py:81
  255.3 331.4 %while.140 = (s32[]{:T(128)}, f32[2,3,256]{2,1,0:T(4,128)S(1)}, f32[2,3,256]{2,1,0:T(4,128)S(1)}, bf16[2,256,64]{1,2,0:T(8,128)(2,1)S(1)}, s32[256]{0:T(256)S(1)...) while((s32[]{:T(128)}, f32[2,3,256]{2,1,0:T(4,128)S(1)}, ...), condition=%wide.region_4.5_spmd.clone, body=%wide.region_1.4_spmd.clone.sunk | while | flops 52502544 | bytes 4024685 | solution.py:138
  586.7 407.8 %while.141 = (s32[]{:T(128)}, f32[2,3,256,64]{2,3,1,0:T(8,128)S(1)}, bf16[2,256,64]{1,2,0:T(8,128)(2,1)S(1)}, bf16[2,256,64]{1,2,0:T(8,128)(2,1)S(1)}, s32[256]{...) while((s32[]{:T(128)}, f32[2,3,256,64]{2,3,1,0:T(8,128)S(1)}, ...), condition=%wide.region_6.7_spmd.clone, body=%wide.region_5.6_spmd.clone.sunk | while | flops 102629904 | bytes 2050460 | solution.py:138
  999.3 333.5 %while.142 = (s32[]{:T(128)}, f32[2,3,256]{2,1,0:T(4,128)S(1)}, f32[2,3,256]{2,1,0:T(4,128)S(1)}, bf16[2,256,64]{1,2,0:T(8,128)(2,1)S(1)}, s32[256]{0:T(256)S(1)...) while((s32[]{:T(128)}, f32[2,3,256]{2,1,0:T(4,128)S(1)}, ...), condition=%wide.region_20.22_spmd.clone, body=%wide.region_17.21_spmd.clone.sunk | while | flops 52502544 | bytes 4024685 | solution.py:138
  1332.9 396.3 %while.143 = (s32[]{:T(128)}, f32[2,3,256,64]{2,3,1,0:T(8,128)S(1)}, bf16[2,256,64]{1,2,0:T(8,128)(2,1)S(1)}, bf16[2,256,64]{1,2,0:T(8,128)(2,1)S(1)}, s32[256]{...) while((s32[]{:T(128)}, f32[2,3,256,64]{2,3,1,0:T(8,128)S(1)}, ...), condition=%wide.region_22.24_spmd.clone, body=%wide.region_21.23_spmd.clone.sunk | while | flops 102629904 | bytes 2050460 | solution.py:138
  1738.2 23.7 reduce-scatter.16.cloned.1.call-done
  1778.8 177.4 %all-gather = bf16[128,12,12]{2,1,0:T(8,128)(2,1)S(1)} all-gather(bf16[1,12,12]{2,1,0:T(8,128)(2,1)S(1)} %bitcast.537), channel_id=1, replica_groups=mesh['ctx'=32,'ep'=4] {'ctx','ep'}, dimensions={0}, use_global_device_ids=true | all-gather | bytes 37152 | tf_op jit(solution)/shard_map/all_gather | solution.py:478
  1996.0 17.1 all-to-all-done.6
  2036.4 42.1 all-gather.13.cloned.1.call-done
  2087.4 155.3 %all-gather.15.cloned.1.call-done = bf16[3,512,1536]{1,2,0:T(8,128)(2,1)} async-done(((bf16[3,512,48]{1,2,0:T(8,128)(2,1)}), bf16[3,512,1536]{1,2,0:T(8,128)(2,1)}) %all-gather.15.cloned.1.call-update) | async-done | bytes 4718608 | tf_op jit(solution)/shard_map/all_gather | solution.py:85
  2322.2 18.1 all-to-all-done.5
  2388.4 10.9 all_gather.75
  2402.7 710.1 %while.144 = (s32[]{:T(128)}, f32[2,3,256,64]{2,3,1,0:T(8,128)S(1)}, bf16[2,256,64]{1,2,0:T(8,128)(2,1)S(1)}, bf16[2,256,64]{1,2,0:T(8,128)(2,1)S(1)}, s32[256]{...) while((s32[]{:T(128)}, f32[2,3,256,64]{2,3,1,0:T(8,128)S(1)}, ...), condition=%wide.region_40.42_spmd.clone, body=%wide.region_39.41_spmd.clone.sunk | while | flops 255459856 | bytes 11100686 | solution.py:138
  3129.1 764.5 %while.145 = (s32[]{:T(128)}, f32[2,3,256,64]{2,3,1,0:T(8,128)S(1)}, bf16[2,256,64]{1,2,0:T(8,128)(2,1)S(1)}, bf16[2,256,64]{1,2,0:T(8,128)(2,1)}, s32[256]{0:T(...) while((s32[]{:T(128)}, f32[2,3,256,64]{2,3,1,0:T(8,128)S(1)}, ...), condition=%wide.region_51.53_spmd.clone, body=%wide.region_50.52_spmd.clone.sunk | while | flops 255459856 | bytes 11100686 | solution.py:138
  3938.0 285.9 %fusion.24 = f32[16,12]{1,0:T(8,128)S(1)} fusion(f32[1536,12]{1,0:T(8,128)S(1)} %convolution_add_fusion.3), kind=kCustom, calls=%all-reduce-scatter | all-reduce-scatter fusion | flops 24577 | bytes 74496
  4229.9 33.2 collective-permute-start.49
  4284.8 12.0 collective-permute-start.42
  4404.6 65.3 %all-reduce.6 = (f32[1536]{0:T(1024)S(1)}, f32[1536]{0:T(1024)S(1)}) all-reduce(f32[1536]{0:T(1024)S(1)} %add.758, f32[1536]{0:T(1024)S(1)} %add.763), channel_id=6, replica_groups=mesh['ctx'=32,'ep'=4] {'ctx','ep'}, use_global_device_ids=true, to_apply=%region_56.58.clone | all-reduce | flops 3072 | bytes 24576
  4474.5 115.1 %reduce-scatter.28.cloned.1.call-done = bf16[384,48]{0,1:T(8,128)(2,1)} async-done(((bf16[384,1536]{0,1:T(8,128)(2,1)}), bf16[384,48]{0,1:T(8,128)(2,1)}) %reduce-scatter.28.cloned.1.call-update) | async-done | bytes 36880 | tf_op jit(solution)/shard_map/reduce_scatter | solution.py:100
  4591.0 166.3 %reduce-scatter.30.cloned.1.call-done = bf16[3,48,512]{2,1,0:T(8,128)(2,1)} async-done(((bf16[3,1536,512]{2,1,0:T(8,128)(2,1)}), bf16[3,48,512]{2,1,0:T(8,128)(2,1)}) %reduce-scatter.30.cloned.1.call-update) | async-done | bytes 147472 | tf_op jit(solution)/shard_map/reduce_scatter | solution.py:103
  4759.0 166.8 %reduce-scatter.32.cloned.1.call-done = bf16[3,48,512]{2,1,0:T(8,128)(2,1)} async-done(((bf16[3,1536,512]{2,1,0:T(8,128)(2,1)}), bf16[3,48,512]{2,1,0:T(8,128)(2,1)}) %reduce-scatter.32.cloned.1.call-update) | async-done | bytes 147472 | tf_op jit(solution)/shard_map/reduce_scatter | solution.py:106
  4927.4 165.3 %reduce-scatter.34.cloned.1.call-done = bf16[3,512,48]{1,2,0:T(8,128)(2,1)} async-done(((bf16[3,512,1536]{1,2,0:T(8,128)(2,1)}), bf16[3,512,48]{1,2,0:T(8,128)(2,1)}) %reduce-scatter.34.cloned.1.call-update) | async-done | bytes 147472 | tf_op jit(solution)/shard_map/reduce_scatter | solution.py:109
  (3818 shorter events, 3392.4 us)
Async XLA Ops:
  7.2 241.4 %all-gather.7.cloned.1.call-start = ((), (), s32[]{:S(2)}) async-start(), calls=%async_computation.19 | async-start | bytes 1216512 | tf_op jit(solution)/shard_map/all_gather | solution.py:79
  7.9 986.6 %all-gather.9.cloned.1.call-start = ((), (), s32[]{:S(2)}) async-start(), calls=%async_computation.20 | async-start | bytes 1216512 | tf_op jit(solution)/shard_map/all_gather | solution.py:82
  8.7 1729.5 %reduce-scatter.14.cloned.1.call-start = ((), (), s32[]{:S(2)}) async-start(), calls=%async_computation.21 | async-start | bytes 983040 | tf_op jit(solution)/shard_map/reduce_scatter | solution.py:278
  997.7 764.3 %reduce-scatter.16.cloned.1.call-start = ((), (), s32[]{:S(2)}) async-start(), calls=%async_computation.25 | async-start | bytes 983040 | tf_op jit(solution)/shard_map/reduce_scatter | solution.py:278
  1732.0 301.0 %all-gather.11.cloned.1.call-start = ((), (), s32[]{:S(2)}) async-start(), calls=%async_computation.22 | async-start | bytes 4866048 | tf_op jit(solution)/shard_map/all_gather | solution.py:83
  1732.6 345.9 %all-gather.13.cloned.1.call-start = ((), (), s32[]{:S(2)}) async-start(), calls=%async_computation.23 | async-start | bytes 4866048 | tf_op jit(solution)/shard_map/all_gather | solution.py:84
  1733.2 509.5 %all-gather.15.cloned.1.call-start = ((), (), s32[]{:S(2)}) async-start(), calls=%async_computation.24 | async-start | bytes 4866048 | tf_op jit(solution)/shard_map/all_gather | solution.py:85
  1775.1 198.9 %all-to-all-start.2 = ((bf16[3,4,48,1536]{3,2,0,1:T(8,128)(2,1)}), bf16[3,4,48,1536]{3,2,0,1:T(8,128)(2,1)S(1)}, u32[]{:S(2)}, u32[]{:S(2)}) async-start(bf16[3,4,48,1536]{3,2,0,1:T(8,128)(2,1)} %copy.144), calls=%async_computation.4 | async-start | bytes 3538944 | tf_op jit(solution)/shard_map/all_to_all | solution.py:305
  2013.1 69.8 %all-to-all-start = ((bf16[3,4,48,1536]{3,2,0,1:T(8,128)(2,1)}), bf16[3,4,48,1536]{3,2,0,1:T(8,128)(2,1)}, u32[]{:S(2)}, u32[]{:S(2)}) async-start(bf16[3,4,48,1536]{3,2,0,1:T(8,128)(2,1)} %copy.135), calls=%async_computation.1 | async-start | bytes 3538944 | tf_op jit(solution)/shard_map/all_to_all | solution.py:305
  2083.0 172.4 %all-to-all-start.4 = ((bf16[3,4,48,1536]{3,2,0,1:T(8,128)(2,1)}), bf16[3,4,48,1536]{3,2,0,1:T(8,128)(2,1)S(1)}, u32[]{:S(2)}, u32[]{:S(2)}) async-start(bf16[3,4,48,1536]{3,2,0,1:T(8,128)(2,1)} %copy.150), calls=%async_computation.6 | async-start | bytes 3538944 | tf_op jit(solution)/shard_map/all_to_all | solution.py:334
  2345.9 2054.5 %reduce-scatter.24.cloned.1.call-start = ((), (), s32[]{:S(2)}) async-start(), calls=%async_computation.29 | async-start | bytes 405504 | tf_op jit(solution)/shard_map/reduce_scatter | solution.py:94
  3900.6 501.2 %reduce-scatter.26.cloned.1.call-start = ((), (), s32[]{:S(2)}) async-start(), calls=%async_computation.30 | async-start | bytes 405504 | tf_op jit(solution)/shard_map/reduce_scatter | solution.py:97
  3901.3 501.7 %reduce-scatter.18.cloned.1.call-start = ((), (), s32[]{:S(2)}) async-start(), calls=%async_computation.26 | async-start | bytes 983040 | tf_op jit(solution)/shard_map/reduce_scatter | solution.py:434
  3904.7 498.4 %reduce-scatter.20.cloned.1.call-start = ((), (), s32[]{:S(2)}) async-start(), calls=%async_computation.27 | async-start | bytes 983040 | tf_op jit(solution)/shard_map/reduce_scatter | solution.py:434
  3908.2 565.0 %reduce-scatter.22.cloned.1.call-start = ((), (), s32[]{:S(2)}) async-start(), calls=%async_computation.28 | async-start | bytes 1216512 | tf_op jit(solution)/shard_map/reduce_scatter | solution.py:91
  3911.9 677.7 %reduce-scatter.28.cloned.1.call-start = ((), (), s32[]{:S(2)}) async-start(), calls=%async_computation.31 | async-start | bytes 1216512 | tf_op jit(solution)/shard_map/reduce_scatter | solution.py:100
  3915.6 841.7 %reduce-scatter.30.cloned.1.call-start = ((), (), s32[]{:S(2)}) async-start(), calls=%async_computation.32 | async-start | bytes 4866048 | tf_op jit(solution)/shard_map/reduce_scatter | solution.py:103
  3922.1 1003.6 %reduce-scatter.32.cloned.1.call-start = ((), (), s32[]{:S(2)}) async-start(), calls=%async_computation.33 | async-start | bytes 4866048 | tf_op jit(solution)/shard_map/reduce_scatter | solution.py:106
  3928.6 1164.1 %reduce-scatter.34.cloned.1.call-start = ((), (), s32[]{:S(2)}) async-start(), calls=%async_computation.34 | async-start | bytes 4866048 | tf_op jit(solution)/shard_map/reduce_scatter | solution.py:109
  4223.9 44.3 collective-permute-start.50
  4226.4 39.9 collective-permute-start.51
  4229.9 40.3 collective-permute-start.49
  4339.5 43.2 collective-permute-start.25
  4349.0 44.8 collective-permute-start.24
  (804 other events, 16214.4 us)
Sparse Core Ops, SparseCore 0:
  9.7 143.4 all-gather.6
  154.8 151.7 all-gather.8
  997.8 30.7 reduce-scatter.13
  1732.1 29.7 reduce-scatter.15
  1763.4 151.3 all-gather.10
  1916.3 162.1 all-gather.12
  2080.2 162.4 all-gather.14
  3900.7 145.5 reduce-scatter.23
  4048.8 156.0 reduce-scatter.25
  4207.4 42.8 reduce-scatter.17
  4253.1 29.8 reduce-scatter.19
  4285.2 144.2 reduce-scatter.21
  4432.0 157.5 reduce-scatter.27
  4591.9 165.4 reduce-scatter.29
  4759.6 166.1 reduce-scatter.31
  4928.0 164.6 reduce-scatter.33
where the time goes:
time: 5150 us; the launch traced here: 5100 us
  starting transfers between devices  2170 us (42%)
  waiting for transfers between devices  1360 us (26%)
  blocking collectives  783 us (15%)
  matrix products  374 us (7%)
  local copies, waits for them, and re-layouts  190 us (4%)
  other arithmetic  190 us (4%)
    ppermute x512, starting transfers between devices, shifted(): return lax.ppermute(value, axis, pairs)  1690 us
    unnamed x3, blocking collectives  418 us
    ppermute x512, waiting for transfers between devices, shifted(): return lax.ppermute(value, axis, pairs)  318 us
    ppermute x128, starting transfers between devices, from_behind(): return lax.ppermute(block, axis, route)  282 us
    all_gather x1, blocking collectives, local(): lax.all_gather(router, ('ctx', 'ep'), axis=0, tiled=True)  177 us
    reduce_scatter x1, waiting for transfers between devices, reduce_grads(): lax.psum_scatter(weight_grads[5].astype(jnp.bfloat16), 'ctx', scatter_dim...  167 us
    reduce_scatter x1, waiting for transfers between devices, reduce_grads(): lax.psum_scatter(weight_grads[4].astype(jnp.bfloat16), 'ctx', scatter_dim...  166 us
    reduce_scatter x1, waiting for transfers between devices, reduce_grads(): lax.psum_scatter(weight_grads[6].astype(jnp.bfloat16), 'ctx', scatter_dim...  165 us
  transfers between devices with their start and end apart: 696, of which 236 were waited for; matrix products, arithmetic and copies ran while one was open for 20% of the time, Pallas kernels for 0%

commit v1 on v0

v1 whole, which is shorter than its diff:
```python
import math

import jax
import jax.numpy as jnp
from jax import lax
from jax.experimental import pallas as pl
from jax.experimental.pallas import tpu as pltpu
from jax.sharding import PartitionSpec as P

HEAD_DIM = 64
HALF = 32
GROUP = 3
KV_DEV = 2
EXP_DEV = 3
EXPERTS = 12
MB = 2
COMBOS = MB * KV_DEV
BLOCK = 256
LANES = GROUP * BLOCK
COVERING = 4.0
EPSILON = 1e-06
MASKED = -1e30
F32 = jnp.float32
BF16 = jnp.bfloat16
CHUNK_OWNERS = (0, 2, 1, 3)


def dot(left, right):
    return jnp.dot(left, right, preferred_element_type=F32)


def dot_rows(left, right):
    return lax.dot_general(left, right, (((0,), (0,)), ((), ())), preferred_element_type=F32)


def dot_columns(left, right):
    return lax.dot_general(left, right, (((1,), (1,)), ((), ())), preferred_element_type=F32)


def gather_ctx(part):
    copies = jnp.broadcast_to(part[None], (lax.axis_size("ctx"), *part.shape))
    return lax.all_to_all(copies, "ctx", 0, 0, tiled=True)


def sum_ctx(parts):
    return jnp.sum(lax.all_to_all(parts, "ctx", 0, 0, tiled=True).astype(F32), axis=0)


def after(value, *others):
    for other in others:
        first = lax.slice(other, (0,) * other.ndim, (1,) * other.ndim).reshape(())
        value = value + (first * 0).astype(value.dtype)
    return value


LINKS = ((1, 1), (2, 1), (0, 1), (2, 3), (0, 3))
GRID = (4, 2, 4)


def grid_place(index):
    return (index // 8, index // 4 % 2, index % 4)


def across_link(value, link):
    axis, distance = link

    def partner(device):
        place = list(grid_place(device))
        place[axis] ^= distance
        return (place[0] * GRID[1] + place[1]) * GRID[2] + place[2]

    size = lax.axis_size("ctx")
    return lax.ppermute(value, "ctx", [(i, partner(i)) for i in range(size)])


def cut(value, axis, start, stop):
    return lax.slice_in_dim(value, start, stop, axis=axis)


def join_halves(mine, theirs, link, place):
    axis, distance = link
    both = [mine, theirs]
    if GRID[axis] == 2 or (distance == 1 and mine.shape[axis] == 1):
        second = place[axis] % 2 == 1
    elif distance == 3:
        second = place[axis] >= 2
    else:
        outer = (place[axis] == 0) | (place[axis] == 3)
        ends, middle = jnp.where(outer, mine, theirs), jnp.where(outer, theirs, mine)
        return jnp.concatenate([cut(ends, axis, 0, 1), middle, cut(ends, axis, 1, 2)], axis=axis)
    return jnp.where(
        second,
        jnp.concatenate(both[::-1], axis=axis),
        jnp.concatenate(both, axis=axis),
    )


def link_of(step, part):
    return LINKS[(step + part) % len(LINKS)]


def link_mask(link):
    axis, distance = link
    return distance * (8, 4, 1)[axis]


def place_masks(part):
    masks = [0]
    for step in range(len(LINKS)):
        masks = masks + [mask ^ link_mask(link_of(step, part)) for mask in masks]
    return masks


def gather_step(parts, step):
    return [
        jnp.concatenate([part, across_link(part, link_of(step, at))])
        for at, part in enumerate(parts)
    ]


def gather_in_place(part, at):
    place = grid_place(lax.axis_index("ctx"))
    part = part[None, None, None]
    for step in range(len(LINKS)):
        link = link_of(step, at)
        part = join_halves(part, across_link(part, link), link, place)
    return part.reshape(-1, part.shape[-1])


def sum_links(pairs):
    for step in reversed(range(len(LINKS))):
        sums = [
            kept.astype(F32) + across_link(sent, link_of(step, at)).astype(F32)
            for at, (kept, sent) in enumerate(pairs)
        ]
        pairs = []
        for total in sums:
            half = total.shape[0] // 2
            total = total.astype(BF16) if step else total
            pairs.append((total[:half], total[half:]))
    return [total[0] for total in sums]


def across_ep(value, distance):
    return lax.ppermute(value, "ep", [(i, i ^ distance) for i in range(4)])


def gather_ep(rows, axis):
    half = jnp.concatenate([rows, across_ep(rows, 2)], axis=axis)
    return jnp.concatenate([half, across_ep(half, 1)], axis=axis)


def finish_sum(kept, received):
    half = kept + received.astype(F32)
    size = half.shape[1] // 2
    return half[:, :size] + across_ep(half[:, size:].astype(BF16), 2).astype(F32)


def sum_ep(rows, axis, sent_as=BF16):
    size = rows.shape[axis] // 4

    kept, sent = cut(rows, axis, 0, 2 * size), cut(rows, axis, 2 * size, 4 * size)
    half = kept.astype(F32) + across_ep(sent.astype(sent_as), 1).astype(F32)
    kept, sent = cut(half, axis, 0, size), cut(half, axis, size, 2 * size)
    return kept + across_ep(sent.astype(sent_as), 2).astype(F32)


def quad_member(device, size, distance):
    planes, plane = 4, size // 4
    slot, place = device // plane, device % plane
    if distance % 2:
        place = plane - 1 - place
    return (slot ^ distance) % planes * plane + place


def quad_block(ctx, size, distance):
    plane = size // 4
    slot, place = ctx // plane, ctx % plane
    if distance % 2:
        place = plane - 1 - place
    return (slot ^ distance) * plane + place


def across_quad(value, distance):
    size = lax.axis_size("ctx")
    return lax.ppermute(
        value, "ctx", [(i, quad_member(i, size, distance)) for i in range(size)]
    )


def swap_quad(parts):
    return [parts[0]] + [across_quad(parts[distance], distance) for distance in range(1, 4)]


def pick(parts, index):
    return lax.dynamic_index_in_dim(parts, index, 0, keepdims=False)


def rms_scale(values):
    return lax.rsqrt(jnp.mean(values * values, axis=-1, keepdims=True) + EPSILON)


def rope_tables(positions):
    inverse = jnp.exp(
        jnp.arange(HALF, dtype=F32) * (-2.0 * math.log(10000.0) / HEAD_DIM)
    )
    angles = inverse[:, None] * positions.astype(F32)[..., None, :]
    return jnp.cos(angles), jnp.sin(angles)


def rotate(values, cosine, sine):
    first, second = values[..., :HALF, :], values[..., HALF:, :]
    return jnp.concatenate(
        [first * cosine - second * sine, second * cosine + first * sine], axis=-2
    )


def unrotate(values, cosine, sine):
    first, second = values[..., :HALF, :], values[..., HALF:, :]
    return jnp.concatenate(
        [first * cosine + second * sine, second * cosine - first * sine], axis=-2
    )


def widen(heads_ref, side, target_ref, offset):
    target_ref[...] = jnp.zeros_like(target_ref)
    for head in range(GROUP):
        target_ref[offset : offset + HEAD_DIM, head * BLOCK : (head + 1) * BLOCK] = heads_ref[
            side, head
        ]


def allowed_pairs(key_block, query_block, key_segments, query_segments, row_ref, col_ref):
    keys = col_ref[:, 0:1] + key_block * BLOCK
    queries = row_ref[...] + query_block * BLOCK
    return (key_segments == query_segments) & (keys <= queries)


def forward_kernel(
    blocks_ref,
    q_ref,
    kv_ref,
    seg_row_ref,
    seg_col_ref,
    row_ref,
    col_ref,
    o_ref,
    lse_ref,
    q_wide,
    top,
    total,
    acc,
):
    def one_side(side, nothing):
        query_block = blocks_ref[side]
        widen(q_ref, side, q_wide, 0)
        top[...] = jnp.full_like(top, MASKED)
        total[...] = jnp.zeros_like(total)
        acc[...] = jnp.zeros_like(acc)
        query_segments = seg_row_ref[side]
        covered = query_segments == COVERING

        def add(block, scores, scale_by, new_top):
            weights = jnp.exp(scores - scale_by)
            shrink = jnp.exp(top[...] - new_top)
            top[...] = new_top
            total[...] = total[...] * shrink + jnp.sum(weights, axis=0, keepdims=True)
            added = dot_rows(kv_ref[block], weights.astype(BF16))[HEAD_DIM:]
            acc[...] = acc[...] * shrink + added

        def edge(block, column):
            scores = dot(kv_ref[block], q_wide[...])
            allowed = allowed_pairs(
                block, query_block, seg_col_ref[column][:, 0:1], query_segments, row_ref, col_ref
            )
            scores = jnp.where(allowed, scores, MASKED)
            new_top = jnp.maximum(top[...], jnp.max(scores, axis=0, keepdims=True))
            add(block, scores, new_top, new_top)

        def inner(block, carry):
            scores = dot(kv_ref[block], q_wide[...])
            new_top = jnp.maximum(top[...], jnp.max(scores, axis=0, keepdims=True))
            add(
                block,
                scores,
                jnp.where(covered, new_top, -MASKED),
                jnp.where(covered, new_top, top[...]),
            )
            return carry

        @pl.when(query_block > 0)
        def _():
            edge(0, COMBOS)

        lax.fori_loop(1, query_block, inner, 0)
        edge(query_block, side)
        lse_ref[side] = top[...] + jnp.log(total[...])
        result = acc[...] / total[...]
        for head in range(GROUP):
            o_ref[side, head] = result[:, head * BLOCK : (head + 1) * BLOCK]
        return nothing

    lax.fori_loop(0, COMBOS, one_side, 0)


def backward_kernel(
    blocks_ref,
    q_ref,
    do_ref,
    kv_ref,
    o_ref,
    lse_ref,
    seg_row_ref,
    seg_col_ref,
    row_ref,
    col_ref,
    cos_ref,
    sin_ref,
    dq_ref,
    dkv_ref,
    q_wide,
    do_wide,
    q_tall,
    do_tall,
    dq_acc,
    dkv_acc,
):
    dkv_acc[...] = jnp.zeros_like(dkv_acc)

    def one_side(side, nothing):
        query_block = blocks_ref[side]
        widen(q_ref, side, q_wide, 0)
        widen(do_ref, side, do_wide, HEAD_DIM)
        for head in range(GROUP):
            at = slice(head * BLOCK, (head + 1) * BLOCK)
            q_tall[at, :] = q_wide[:, at].astype(F32).T.astype(BF16)
            do_tall[at, :] = do_wide[:, at].astype(F32).T.astype(BF16)
        dq_acc[...] = jnp.zeros_like(dq_acc)
        query_segments = seg_row_ref[side]
        lse = lse_ref[side]
        covered_lse = jnp.where(query_segments == COVERING, lse, -MASKED)
        delta = jnp.concatenate(
            [
                jnp.sum(
                    o_ref[side, head] * do_ref[side, head].astype(F32), axis=0, keepdims=True
                )
                for head in range(GROUP)
            ],
            axis=1,
        )

        def add(block, scores, scale_by):
            weights = jnp.exp(scores - scale_by)
            grad_weights = dot(kv_ref[block], do_wide[...])
            grad_scores = (weights * (grad_weights - delta)).astype(BF16)
            dkv_acc[block] += dot(grad_scores, q_tall[...]) + dot(
                weights.astype(BF16), do_tall[...]
            )
            dq_acc[...] += dot_rows(kv_ref[block], grad_scores)[:HEAD_DIM]

        def edge(block, column):
            scores = dot(kv_ref[block], q_wide[...])
            allowed = allowed_pairs(
                block, query_block, seg_col_ref[column][:, 0:1], query_segments, row_ref, col_ref
            )
            add(block, jnp.where(allowed, scores, MASKED), lse)

        def inner(block, carry):
            add(block, dot(kv_ref[block], q_wide[...]), covered_lse)
            return carry

        @pl.when(query_block > 0)
        def _():
            edge(0, COMBOS)

        lax.fori_loop(1, query_block, inner, 0)
        edge(query_block, side)
        for head in range(GROUP):
            at = slice(head * BLOCK, (head + 1) * BLOCK)
            grad = unrotate(dq_acc[:, at], cos_ref[side], sin_ref[side])
            dq_ref[side, head] = (grad * (1.0 / math.sqrt(HEAD_DIM))).astype(BF16)
        return nothing

    lax.fori_loop(0, COMBOS, one_side, 0)
    dkv_ref[...] = dkv_acc[...].astype(BF16)


def experts_kernel(
    places_ref,
    ep_ref,
    tokens_ref,
    cotangent_ref,
    gates_ref,
    *refs,
):
    halves, refs = refs[:8], refs[8:]
    grad_kept, grad_sent, out_kept, out_sent, pre_ref, hidden_ref = refs[:6]
    weights, grad_acc, out_acc, gate_acc, arrived = refs[6:]
    quarter = hidden_ref.shape[2]
    rows = tokens_ref.shape[0]
    block_rows = halves[0].shape[1]
    width = tokens_ref.shape[1]

    def fetch(q):
        for half in range(2):
            source = halves[2 * q + half]
            for at in range(source.shape[0]):
                start = places_ref[q, half * source.shape[0] + at] * block_rows
                start = pl.multiple_of(start, 16)
                pltpu.make_async_copy(
                    source.at[at],
                    weights.at[q % 2, pl.ds(start, block_rows)],
                    arrived.at[q % 2],
                ).start()

    fetch(0)
    gate_acc[...] = jnp.zeros_like(gate_acc)
    for q in range(4):
        if q < 3:
            fetch(q + 1)
        pltpu.make_async_copy(weights.at[q % 2], weights.at[q % 2], arrived.at[q % 2]).wait()
        weights_in = weights[q % 2, :, : 2 * quarter]
        weights_out = weights[q % 2, :, 2 * quarter :]
        grad_hidden = dot(cotangent_ref[...], weights_out)
        pre = dot(tokens_ref[...], weights_in)
        gate_pre, up_pre = pre[:, :quarter], pre[:, quarter:]
        sigmoid = 1.0 / (1.0 + jnp.exp(-gate_pre))
        activated = gate_pre * sigmoid
        hidden = activated * up_pre
        products = grad_hidden * hidden
        tiles = [(tile, (q * quarter // 128 + tile) // 4) for tile in range(quarter // 128)]
        gates = jnp.concatenate(
            [
                jnp.broadcast_to(gates_ref[:, expert : expert + 1], (rows, 128))
                for _, expert in tiles
            ],
            axis=1,
        )
        for tile, expert in tiles:
            gate_acc[expert] += products[:, tile * 128 : (tile + 1) * 128]
        gated_hidden = (gates * hidden).astype(BF16)
        grad_hidden = gates * grad_hidden
        pre_ref[q, :, :quarter] = (
            grad_hidden * up_pre * sigmoid * (1.0 + gate_pre * (1.0 - sigmoid))
        ).astype(BF16)
        pre_ref[q, :, quarter:] = (grad_hidden * activated).astype(BF16)
        hidden_ref[q] = gated_hidden
        grad = dot_columns(pre_ref[q], weights_in)
        out = dot_columns(gated_hidden, weights_out)
        if q == 0:
            grad_acc[...] = grad
            out_acc[...] = out
        elif q < 3:
            grad_acc[...] += grad
            out_acc[...] += out
        else:
            for batch in range(MB):
                kept = slice(batch * BLOCK, batch * BLOCK + BLOCK // 2)
                sent = slice(batch * BLOCK + BLOCK // 2, (batch + 1) * BLOCK)
                grad_kept[batch, :, :width] = grad_acc[kept] + grad[kept]
                grad_sent[batch, :, :width] = (grad_acc[sent] + grad[sent]).astype(BF16)
                out_kept[batch] = out_acc[kept] + out[kept]
                out_sent[batch] = (out_acc[sent] + out[sent]).astype(BF16)
    columns = lax.broadcasted_iota(jnp.int32, (rows, 128), 1) - ep_ref[0] * EXP_DEV
    message = jnp.zeros((rows, 128), F32)
    for expert in range(EXP_DEV):
        total = jnp.sum(gate_acc[expert], axis=1, keepdims=True)
        high = total.astype(BF16).astype(F32)
        message = jnp.where(columns == expert, high, message)
        message = jnp.where(columns == expert + EXPERTS, total - high, message)
    for batch in range(MB):
        start = batch * BLOCK
        grad_kept[batch, :, width:] = message[start : start + BLOCK // 2]
        grad_sent[batch, :, width:] = message[start + BLOCK // 2 : start + BLOCK].astype(BF16)


def expert_grads_kernel(
    places_ref, tokens_ref, cotangent_ref, pre_ref, hidden_ref, kept_ref, sent_ref, scratch
):
    half, block_rows, _ = kept_ref.shape
    planes, quarter = 4, hidden_ref.shape[2]
    rows = tokens_ref.shape[1] // planes
    blocks = rows // block_rows
    for plane in range(planes):
        at = slice(plane * rows, (plane + 1) * rows)
        scratch[:, : 2 * quarter] = dot_rows(tokens_ref[:, at], pre_ref[0]).astype(BF16)
        scratch[:, 2 * quarter :] = dot_rows(cotangent_ref[:, at], hidden_ref[0]).astype(BF16)
        for block in range(blocks):
            place = places_ref[plane * blocks + block]
            value = scratch[block * block_rows : (block + 1) * block_rows, :]

            @pl.when(place < half)
            def _():
                kept_ref[place] = value

            @pl.when(place >= half)
            def _():
                sent_ref[place - half] = value


SMEM_SPEC = pl.BlockSpec(memory_space=pltpu.SMEM)
VMEM_SPEC = pl.BlockSpec(memory_space=pltpu.VMEM)
HEADS_SHAPE = (COMBOS, GROUP, HEAD_DIM, BLOCK)


ANY_SPEC = pl.BlockSpec(memory_space=pl.ANY)


def run_experts(places, ep, tokens, cotangent, gates, halves):
    rows, width = tokens.shape
    _, block_rows, columns = halves[0].shape
    quarter = columns // 3
    kept_rows = (MB, BLOCK // 2)
    return pl.pallas_call(
        experts_kernel,
        out_shape=(
            jax.ShapeDtypeStruct((*kept_rows, width + 128), F32),
            jax.ShapeDtypeStruct((*kept_rows, width + 128), BF16),
            jax.ShapeDtypeStruct((*kept_rows, width), F32),
            jax.ShapeDtypeStruct((*kept_rows, width), BF16),
            jax.ShapeDtypeStruct((4, rows, 2 * quarter), BF16),
            jax.ShapeDtypeStruct((4, rows, quarter), BF16),
        ),
        in_specs=[SMEM_SPEC] * 2 + [VMEM_SPEC] * 3 + [ANY_SPEC] * 8,
        out_specs=(VMEM_SPEC,) * 6,
        scratch_shapes=[
            pltpu.VMEM((2, width, columns), BF16),
            pltpu.VMEM((rows, width), F32),
            pltpu.VMEM((rows, width), F32),
            pltpu.VMEM((EXP_DEV, rows, 128), F32),
            pltpu.SemaphoreType.DMA((2,)),
        ],
        compiler_params=pltpu.CompilerParams(vmem_limit_bytes=50 * 1024 * 1024),
        cost_estimate=pl.CostEstimate(
            flops=16 * rows * width * columns,
            bytes_accessed=30 * 1024 * 1024,
            transcendentals=4 * rows * quarter,
        ),
        name="run_experts",
    )(places, ep, tokens, cotangent, gates, *halves)


def expert_grads(q, places, tokens, cotangent, pre, hidden, block_rows):
    rows, width = tokens.shape
    quarter = hidden.shape[2]
    half = jax.ShapeDtypeStruct((width // block_rows // 2, block_rows, 3 * quarter), BF16)
    whole = pl.BlockSpec((rows, width), lambda i: (0, 0))
    return pl.pallas_call(
        expert_grads_kernel,
        grid=(1,),
        out_shape=(half, half),
        in_specs=[
            SMEM_SPEC,
            whole,
            whole,
            pl.BlockSpec((1, rows, 2 * quarter), lambda i: (q, 0, 0)),
            pl.BlockSpec((1, rows, quarter), lambda i: (q, 0, 0)),
        ],
        out_specs=(pl.BlockSpec(half.shape, lambda i: (0, 0, 0)),) * 2,
        scratch_shapes=[pltpu.VMEM((width // 4, 3 * quarter), BF16)],
        compiler_params=pltpu.CompilerParams(vmem_limit_bytes=40 * 1024 * 1024),
        cost_estimate=pl.CostEstimate(
            flops=6 * rows * width * quarter,
            bytes_accessed=8 * 1024 * 1024,
            transcendentals=0,
        ),
        name="expert_grads",
    )(places, tokens, cotangent, pre, hidden)


def attend(blocks, queries, keys_values, *places):
    steps = 2 * keys_values.shape[0] + 2
    return pl.pallas_call(
        forward_kernel,
        out_shape=(
            jax.ShapeDtypeStruct(HEADS_SHAPE, F32),
            jax.ShapeDtypeStruct((COMBOS, 1, LANES), F32),
        ),
        in_specs=[SMEM_SPEC] + [VMEM_SPEC] * 6,
        out_specs=(VMEM_SPEC, VMEM_SPEC),
        scratch_shapes=[
            pltpu.VMEM((2 * HEAD_DIM, LANES), BF16),
            pltpu.VMEM((1, LANES), F32),
            pltpu.VMEM((1, LANES), F32),
            pltpu.VMEM((HEAD_DIM, LANES), F32),
        ],
        compiler_params=pltpu.CompilerParams(vmem_limit_bytes=32 * 1024 * 1024),
        cost_estimate=pl.CostEstimate(
            flops=steps * 8 * BLOCK * LANES * HEAD_DIM,
            bytes_accessed=4 * 1024 * 1024,
            transcendentals=steps * BLOCK * LANES,
        ),
        name="attend",
    )(blocks, queries, keys_values, *places)


def attend_back(blocks, queries, grads, keys_values, mixed, lse, *places):
    steps = 2 * keys_values.shape[0] + 2
    return pl.pallas_call(
        backward_kernel,
        out_shape=(
            jax.ShapeDtypeStruct(HEADS_SHAPE, BF16),
            jax.ShapeDtypeStruct(keys_values.shape, BF16),
        ),
        in_specs=[SMEM_SPEC] + [VMEM_SPEC] * 11,
        out_specs=(VMEM_SPEC, VMEM_SPEC),
        scratch_shapes=[
            pltpu.VMEM((2 * HEAD_DIM, LANES), BF16),
            pltpu.VMEM((2 * HEAD_DIM, LANES), BF16),
            pltpu.VMEM((LANES, 2 * HEAD_DIM), BF16),
            pltpu.VMEM((LANES, 2 * HEAD_DIM), BF16),
            pltpu.VMEM((HEAD_DIM, LANES), F32),
            pltpu.VMEM(keys_values.shape, F32),
        ],
        compiler_params=pltpu.CompilerParams(vmem_limit_bytes=40 * 1024 * 1024),
        cost_estimate=pl.CostEstimate(
            flops=steps * 20 * BLOCK * LANES * HEAD_DIM,
            bytes_accessed=6 * 1024 * 1024,
            transcendentals=steps * BLOCK * LANES,
        ),
        name="attend_back",
    )(blocks, queries, grads, keys_values, mixed, lse, *places)


def local(
    inputs,
    cotangent,
    segments,
    routes,
    attn_gain,
    w_query,
    key_weight,
    value_weight,
    w_out,
    ffn_gain,
    router,
    w_gate,
    w_up,
    w_down,
):
    ctx_count = lax.axis_size("ctx")
    ctx = lax.axis_index("ctx")
    ep = lax.axis_index("ep")
    slot = ctx // (ctx_count // 4)
    blocks = jnp.stack([quad_block(ctx, ctx_count, distance) for distance in range(4)])
    rows_weight = w_query.shape[0]
    token_rows = inputs.shape[1]
    width = inputs.shape[2]
    hidden_width = w_gate.shape[2]
    width_query = w_query.shape[1]
    width_key = key_weight.shape[1]
    width_joined = width_query + 2 * width_key
    side_start = width_joined
    small_rows = attn_gain.shape[0]
    owners = [ep ^ owner for owner in CHUNK_OWNERS]

    in_width = EXP_DEV * hidden_width
    quarter = in_width // 4
    expert_rows = [
        jnp.concatenate([w_gate[e] for e in range(EXP_DEV)], axis=1),
        jnp.concatenate([w_up[e] for e in range(EXP_DEV)], axis=1),
        jnp.concatenate([w_down[e].T for e in range(EXP_DEV)], axis=1),
    ]
    weight_parts = [
        jnp.concatenate([rows[:, q * quarter : (q + 1) * quarter] for rows in expert_rows], axis=1)
        for q in range(4)
    ]
    expert_ids = jnp.arange(EXPERTS, dtype=jnp.int32)
    chosen_own = jnp.any(routes[..., None] == expert_ids, axis=2).astype(BF16)
    small_own = jnp.concatenate([attn_gain[:, None], ffn_gain[:, None], router], axis=1)
    small_width = small_own.shape[1]
    small_parts = gather_ep(
        jnp.pad(small_own, ((0, 16 - small_rows), (0, 128 - small_width)))[None], 0
    )[:, :small_rows, :small_width]
    natural = [pick(jnp.asarray(CHUNK_OWNERS), ep ^ part) for part in range(4)]
    small_group = jnp.concatenate([pick(small_parts, part) for part in natural])
    chosen = (
        gather_ep(jnp.pad(chosen_own, ((0, 0), (0, 0), (0, 128 - EXPERTS))), 1)[..., :EXPERTS]
        .reshape(MB * BLOCK, EXPERTS)
    ) > 0
    segment_parts = segments.reshape(MB, 4, token_rows).transpose(1, 0, 2)
    segments_here = jnp.stack([pick(segment_parts, owner) for owner in owners], axis=1)
    seg_width = -(-MB * BLOCK // rows_weight)
    seg_part = jnp.pad(
        segments_here.reshape(-1).astype(BF16), (0, seg_width * rows_weight - MB * BLOCK)
    ).reshape(rows_weight, seg_width)
    side_part = jnp.concatenate([small_group, seg_part], axis=1)
    joined_part = jnp.concatenate(
        [
            w_query,
            key_weight,
            value_weight,
            jnp.pad(side_part, ((0, 0), (0, 128 - side_part.shape[1]))),
        ],
        axis=1,
    )
    inputs_all = gather_ep(inputs, 1).reshape(MB * BLOCK, width)
    joined_all = gather_ctx(after(joined_part, inputs_all))
    joined = joined_all[:, :, :width_joined].reshape(width, width_joined)
    side_all = joined_all[:, :, side_start:].reshape(width, 128)
    experts = [after(part, joined_all)[None] for part in weight_parts]
    w_out_all = gather_in_place(after(w_out.T, joined_all), 4)
    for step in range(4):
        experts = gather_step(experts, step)
    expert_halves = [
        half
        for at, part in enumerate(experts)
        for half in (part, across_link(part, link_of(4, at)))
    ]
    masks = jnp.asarray([place_masks(part) for part in range(4)], jnp.int32)
    expert_places = masks ^ ctx
    grad_places = jnp.stack(
        [
            jnp.asarray([place_masks(part).index(mask) for mask in range(ctx_count)], jnp.int32)[
                jnp.arange(ctx_count, dtype=jnp.int32) ^ ctx
            ]
            for part in range(4)
        ]
    )
    gain_one = side_all[:, 0].astype(F32)
    gain_two = side_all[:, 1].astype(F32)
    router_full = side_all[:, 2 : 2 + EXPERTS]
    seg_all = (
        joined_all[:, :, side_start + small_width : side_start + side_part.shape[1]]
        .reshape(ctx_count, -1)[:, : MB * BLOCK]
        .reshape(ctx_count, MB, BLOCK)
        .astype(F32)
    )
    cotangent_all = gather_ep(cotangent, 1).reshape(MB * BLOCK, width)

    offsets = (
        jnp.stack(owners)[:, None] * token_rows + jnp.arange(token_rows, dtype=jnp.int32)
    ).reshape(BLOCK)
    cosines, sines = rope_tables(blocks[:, None] * BLOCK + offsets)
    cosine_both, sine_both = jnp.tile(cosines[0], (1, MB)), jnp.tile(sines[0], (1, MB))

    def by_combo(heads):
        rows = heads.shape[0] // KV_DEV
        parts = heads.reshape(KV_DEV, rows, MB, BLOCK).transpose(2, 0, 1, 3)
        return parts.reshape(COMBOS, rows, BLOCK)

    def from_combos(parts):
        rows = parts.shape[1]
        parts = parts.reshape(MB, KV_DEV, rows, BLOCK).transpose(1, 2, 0, 3)
        return parts.reshape(KV_DEV * rows, MB * BLOCK)

    def to_attention(heads):
        parts = by_combo(heads).reshape(HEADS_SHAPE)
        return jnp.stack(swap_quad([pick(parts, slot ^ distance) for distance in range(4)]))

    def from_attention(parts):
        parts = jnp.stack(swap_quad([parts[distance] for distance in range(4)]))
        parts = jnp.stack([pick(parts, slot ^ combo) for combo in range(COMBOS)])
        return from_combos(parts.reshape(COMBOS, GROUP * HEAD_DIM, BLOCK))

    values = inputs_all.astype(F32)
    scale_one = rms_scale(values)
    normal_one = values * scale_one
    normed = (normal_one * gain_one).astype(BF16)
    projected = jnp.einsum("td,dc->ct", normed, joined, preferred_element_type=F32)

    def turned(start, stop):
        heads = projected[start:stop].reshape(-1, HEAD_DIM, MB * BLOCK)
        return rotate(heads, cosine_both, sine_both).astype(BF16).reshape(-1, MB * BLOCK)

    keys = by_combo(turned(width_query, width_query + width_key))
    key_values = jnp.concatenate(
        [keys, by_combo(projected[width_query + width_key :].astype(BF16))], axis=1
    ).transpose(0, 2, 1)
    sent = jnp.broadcast_to(
        key_values[:, None], (COMBOS, ctx_count // COMBOS, BLOCK, 2 * HEAD_DIM)
    ).reshape(ctx_count, BLOCK, 2 * HEAD_DIM)
    keys_values = lax.all_to_all(sent, "ctx", 0, 0, tiled=True)
    queries = to_attention(turned(0, width_query) * jnp.asarray(1.0 / math.sqrt(HEAD_DIM), BF16))
    seg_here = pick(seg_all.transpose(1, 0, 2), slot // KV_DEV)
    seg_sides = jnp.stack([pick(seg_here, blocks[side]) for side in range(COMBOS)])
    seg_rows = jnp.tile(seg_sides, (1, GROUP))[:, None, :]
    seg_columns = jnp.broadcast_to(
        jnp.concatenate([seg_sides, seg_here[:1]])[:, :, None], (COMBOS + 1, BLOCK, 128)
    )
    offset_row = jnp.tile(offsets, GROUP)[None, :]
    offset_column = jnp.broadcast_to(offsets[:, None], (BLOCK, 128))
    places = (seg_rows, seg_columns, offset_row, offset_column)
    mixed_parts, lse = attend(
        after(blocks, cotangent_all, chosen.astype(F32), *experts), queries, keys_values, *places
    )
    mixed = from_attention(mixed_parts.astype(BF16))

    attn = jnp.einsum("ht,dh->td", mixed, w_out_all, preferred_element_type=F32)
    attn = sum_ep(attn.reshape(MB, BLOCK, width), 1)
    residual = inputs.astype(F32) + attn
    scale_two = rms_scale(residual)
    normal_two = residual * scale_two
    tokens = (normal_two * gain_two).astype(BF16)
    tokens_all = gather_ep(tokens, 1).reshape(MB * BLOCK, width)

    logits = dot(tokens_all, router_full)
    gates = jax.nn.softmax(jnp.where(chosen, logits, MASKED), axis=-1)
    gates_own = gates.reshape(MB, BLOCK, EXPERTS)[:, :token_rows]
    gates_here = lax.dynamic_slice_in_dim(gates, ep * EXP_DEV, EXP_DEV, axis=1)
    grad_kept, grad_sent, out_kept, out_sent, grad_pre, gated_hidden = run_experts(
        expert_places,
        ep.astype(jnp.int32)[None],
        tokens_all,
        cotangent_all,
        jnp.pad(gates_here, ((0, 0), (0, 128 - EXP_DEV))),
        expert_halves,
    )
    received = across_ep(grad_sent, 1)
    message = finish_sum(grad_kept, received)
    grad_places = after(grad_places, received)
    grad_parts = sum_links(
        [
            expert_grads(
                q, grad_places[q], tokens_all, cotangent_all, grad_pre, gated_hidden, rows_weight
            )
            for q in range(4)
        ]
    )
    outputs = (residual + finish_sum(out_kept, across_ep(out_sent, 1))).astype(BF16)

    grad_gates = (
        message[..., width : width + EXPERTS]
        + message[..., width + EXPERTS : width + 2 * EXPERTS]
    )
    grad_logits = (
        gates_own * (grad_gates - jnp.sum(gates_own * grad_gates, axis=-1, keepdims=True))
    ).astype(BF16)
    grad_tokens = message[..., :width] + jnp.einsum(
        "bte,de->btd", grad_logits, router_full, preferred_element_type=F32
    )
    grad_router = jnp.einsum("btd,bte->de", tokens, grad_logits, preferred_element_type=F32)
    grad_gain_two = jnp.sum(grad_tokens * normal_two, axis=(0, 1))
    scaled = grad_tokens * gain_two
    grad_residual = cotangent.astype(F32) + scale_two * (
        scaled - normal_two * jnp.mean(scaled * normal_two, axis=-1, keepdims=True)
    )
    grad_attn = gather_ep(grad_residual.astype(BF16), 1).reshape(MB * BLOCK, width)
    grad_mixed = jnp.einsum(
        "td,dh->ht", grad_attn, w_out_all, preferred_element_type=F32
    ).astype(BF16)
    grad_mixed = to_attention(grad_mixed)

    small_grads = jnp.concatenate([grad_gain_two[:, None], grad_router], axis=1)
    small_high = lax.reduce_precision(small_grads, 8, 7)
    small_count = small_grads.shape[1]
    grad_out = jnp.einsum("td,ht->dh", grad_attn, mixed, preferred_element_type=F32)
    grad_out = jnp.concatenate(
        [
            grad_out.astype(BF16),
            small_high.astype(BF16),
            (small_grads - small_high).astype(BF16),
            jnp.zeros((width, 128 - 2 * small_count), BF16),
        ],
        axis=1,
    )
    blocks = after(blocks, grad_out, outputs)
    grad_out = sum_ctx(grad_out.reshape(ctx_count, rows_weight, width_query + 128))
    small_grads = (
        grad_out[:, width_query : width_query + small_count]
        + grad_out[:, width_query + small_count : width_query + 2 * small_count]
    )
    grad_out = grad_out[:, :width_query].T

    grad_queries, grad_keys_values = attend_back(
        blocks,
        queries,
        grad_mixed,
        keys_values,
        mixed_parts,
        lse,
        *places,
        cosines,
        sines,
    )
    received = lax.all_to_all(grad_keys_values, "ctx", 0, 0, tiled=True).astype(F32)
    received = jnp.sum(
        received.reshape(COMBOS, ctx_count // COMBOS, BLOCK, 2 * HEAD_DIM), axis=1
    ).transpose(0, 2, 1)
    grad_query = from_attention(grad_queries)
    grad_key = unrotate(received[:, :HEAD_DIM], cosines[0], sines[0])
    grad_kv = jnp.concatenate(
        [
            from_combos(grad_key.astype(BF16)),
            from_combos(received[:, HEAD_DIM:].astype(BF16)),
        ]
    )
    grad_partial = dot_rows(
        jnp.concatenate([grad_query, grad_kv]), joined.T
    )
    grad_normed = sum_ep(grad_partial.reshape(MB, BLOCK, width), 1)
    values = inputs.astype(F32)
    scale_own = rms_scale(values)
    normal_own = values * scale_own
    scaled = grad_normed * gain_one
    input_grads = (
        grad_residual
        + scale_own
        * (scaled - normal_own * jnp.mean(scaled * normal_own, axis=-1, keepdims=True))
    ).astype(BF16)

    grad_joined = jnp.concatenate([grad_query, grad_kv])
    grad_joined = jnp.einsum("td,ct->dc", normed, grad_joined, preferred_element_type=F32)
    grad_joined = sum_ctx(
        grad_joined.astype(BF16).reshape(ctx_count, rows_weight, width_joined)
    )
    grad_w_query = grad_joined[:, :width_query]
    grad_w_kv = grad_joined[:, width_query:]
    grad_gain_one = jnp.sum(
        grad_joined * joined_part[:, :width_joined].astype(F32), axis=1, keepdims=True
    ) / side_part[:, :1].astype(F32)
    small_grads = jnp.concatenate([grad_gain_one, small_grads], axis=1)
    small_grads = jnp.pad(small_grads, ((0, 0), (0, 128 - 1 - small_count)))
    small_grads = small_grads.reshape(4, small_rows, 128)
    small_grads = jnp.stack([pick(small_grads, owner) for owner in owners])
    small_grads = sum_ep(small_grads, 0, F32)[0, :, : 1 + small_count]
    def by_expert(which):
        at = slice(which * quarter, (which + 1) * quarter)
        grad = jnp.concatenate([part[:, at] for part in grad_parts], axis=1)
        return jnp.stack(
            [grad[:, e * hidden_width : (e + 1) * hidden_width] for e in range(EXP_DEV)]
        )

    return (
        outputs,
        input_grads,
        small_grads[:, 0],
        grad_w_query,
        grad_w_kv[:, :width_key],
        grad_w_kv[:, width_key:],
        grad_out,
        small_grads[:, 1],
        small_grads[:, 2:],
        by_expert(0),
        by_expert(1),
        by_expert(2).transpose(0, 2, 1),
    )


def solution(mesh):
    rows = P(None, ("ctx", "ep"), None)
    shared = P(("ctx", "ep"))
    weight = P("ctx", "ep")
    out_weight = P("ep", "ctx")
    expert = P("ep", "ctx", None)
    down = P("ep", None, "ctx")
    router = P(("ctx", "ep"), None)
    return jax.shard_map(
        local,
        mesh=mesh,
        in_specs=(
            rows,
            rows,
            P(None, "ctx"),
            rows,
            shared,
            weight,
            weight,
            weight,
            out_weight,
            shared,
            router,
            expert,
            expert,
            down,
        ),
        out_specs=(
            rows,
            rows,
            shared,
            weight,
            weight,
            weight,
            out_weight,
            shared,
            router,
            expert,
            expert,
            down,
        ),
        check_vma=False,
    )
```

time: 5150 us -> 673 us (0.13)
  starting transfers between devices: 2170 us -> 167 us
  waiting for transfers between devices: 1360 us -> 147 us
  blocking collectives: 783 us -> 0 us
  matrix products: 374 us -> 11.1 us
  Pallas kernels: 0 us -> 133 us
  other arithmetic: 190 us -> 82.3 us
  local copies, waits for them, and re-layouts: 190 us -> 105 us
    ppermute x640 -> x79, starting transfers between devices: 1970 us -> 126 us  [the longest x45 63 us: across_link(): return lax.ppermute(value, 'ctx', [(i, partner(i)) for i in range(size)])]
    reduce_scatter x11 -> x0, waiting for transfers between devices: 637 us -> none  [the longest x1 167 us: reduce_grads(): lax.psum_scatter(weight_grads[5].astype(jnp.bfloat16), 'ctx', scatter_dim...]
    unnamed x3 -> x0, blocking collectives: 418 us -> none
    all_gather x7 -> x0, blocking collectives: 365 us -> none  [the longest x1 177 us: local(): lax.all_gather(router, ('ctx', 'ep'), axis=0, tiled=True)]
    dot_general x484 -> x9, matrix products: 374 us -> 11.1 us  [the longest x1 2.93 us: local(): jnp.einsum('td,ct->dc', normed, grad_joined, preferred_element_type=F32)]
    ppermute x640 -> x79, waiting for transfers between devices: 448 us -> 125 us  [the longest x45 61.1 us: across_link(): return lax.ppermute(value, 'ctx', [(i, partner(i)) for i in range(size)])]
    all_gather x5 -> x0, waiting for transfers between devices: 197 us -> none  [the longest x1 155 us: fetch_weights(): lax.all_gather(local_weights[6], 'ctx', axis=2, tiled=True)]
    unnamed x32 -> x0, starting transfers between devices: 158 us -> none
  transfers between devices with their start and end apart: 696 -> 84, of which waited for: 236 -> 22; matrix products, arithmetic and copies ran while one was open for 20% -> 24% of each run, Pallas kernels for 0% -> 16%
where the time goes in v1:
time: 673 us; the launch traced here: 663 us
  starting transfers between devices  167 us (25%)
  waiting for transfers between devices  147 us (22%)
  Pallas kernels  133 us (20%)
  local copies, waits for them, and re-layouts  105 us (16%)
  other arithmetic  82.3 us (12%)
  between operations  18.1 us (3%)
  matrix products  11.1 us (2%)
    ppermute x45, starting transfers between devices, across_link(): return lax.ppermute(value, 'ctx', [(i, partner(i)) for i in range(size)])  63 us
    ppermute x45, waiting for transfers between devices, across_link(): return lax.ppermute(value, 'ctx', [(i, partner(i)) for i in range(size)])  61.1 us
    ppermute x22, waiting for transfers between devices, across_ep(): return lax.ppermute(value, 'ep', [(i, i ^ distance) for i in range(4)])  58.7 us
    pallas_call x1, Pallas kernels, attend_back(): pl.pallas_call(backward_kernel, out_shape=(jax.ShapeDtypeStruct(HEADS_SHA...  45.1 us
    ppermute x12, starting transfers between devices, across_quad(): lax.ppermute(value, 'ctx', [(i, quad_member(i, size, distance)) for i in...  42.2 us
    pallas_call x1, Pallas kernels, attend(): pl.pallas_call(forward_kernel, out_shape=(jax.ShapeDtypeStruct(HEADS_SHAP...  41 us
    unnamed x340, local copies, waits for them, and re-layouts  39.8 us
    pallas_call x1, Pallas kernels, run_experts(): pl.pallas_call(experts_kernel, out_shape=(jax.ShapeDtypeStruct((*kept_row...  27.4 us
  transfers between devices with their start and end apart: 84, of which 22 were waited for; matrix products, arithmetic and copies ran while one was open for 24% of the time, Pallas kernels for 16%

profile of v1, /device:TPU:26, one launch (start us, length us, event | category | flops | bytes accessed | tf_op | source)
XLA Modules:
  0.0 663.2 jit_solution(9125958158138016881)
XLA Ops:
  34.4 9.4 %all-to-all-start = ((bf16[32,48,768]{2,1,0:T(8,128)(2,1)}), bf16[32,48,768]{2,1,0:T(8,128)(2,1)}, u32[]{:S(2)}, u32[]{:S(2)}) async-start(bf16[32,48,768]{2,1,0:T(8,128)(2,1)} %broadcast_in_dim.28), calls=%async_computation | async-start | bytes 4718592 | tf_op jit(solution)/shard_map/all_to_all | solution.py:42
  53.7 21.9 %all-to-all-done = bf16[32,48,768]{2,1,0:T(8,128)(2,1)} async-done(((bf16[32,48,768]{2,1,0:T(8,128)(2,1)}), bf16[32,48,768]{2,1,0:T(8,128)(2,1)}, u32[]{:S(2)}, u32[]{:S(2)}) %all-to-all-start) | async-done | bytes 2359328 | tf_op jit(solution)/shard_map/all_to_all | solution.py:42
  96.0 7.1 %all-to-all-start.1 = ((bf16[32,256,128]{2,1,0:T(8,128)(2,1)}), bf16[32,256,128]{2,1,0:T(8,128)(2,1)S(1)}, u32[]{:S(2)}, u32[]{:S(2)}) async-start(bf16[32,256,128]{2,1,0:T(8,128)(2,1)} %bitcast.323), calls=%async_computation.1 | async-start | bytes 4194304 | tf_op jit(solution)/shard_map/all_to_all | solution.py:773
  108.5 13.4 %collective-permute-start.9 = (bf16[3,64,256]{2,1,0:T(8,128)(2,1)}, bf16[3,64,256]{2,1,0:T(8,128)(2,1)S(1)}, u32[]{:S(2)}, u32[]{:S(2)}) collective-permute-start(bf16[3,64,256]{2,1,0:T(8,128)(2,1)} %get-tuple-element.113), channel_id=1, source_target_pairs={{0,64},{4,68},{8,72},{12,76},{16,80},{20,84},{24,88},{28,92},{32,9... | collective-permute-start | bytes 294920 | tf_op jit(solution)/shard_map/ppermute | solution.py:186
  187.8 41.0 %attend.1 = (f32[4,3,64,256]{3,2,1,0:T(8,128)S(1)}, f32[4,1,768]{2,1,0:T(1,128)S(1)}) custom-call(s32[4]{0:T(128)S(1)} %add_add_fusion.2.blocks_ref, bf16[4,3,64,256]{3,2,1,0:T(8,128)(2,1)S(1)} %pad_maximum_fusion.16.q_ref, bf16[32,256,128]{2,1,0:T(8,128)(2,1)S(1)} %all-to-all-done.1.kv_ref, f32[4,1,768]{2,1,0:T(1,128)S(1)} %copy.282.seg_row_ref, ...), custom_call_target="tpu_custom_call" | custom-call | flops 6643777536 | bytes 4194304 | tf_op jit(solution)/shard_map/attend/pallas_call | solution.py:573
  231.7 5.1 collective-permute-start.13
  259.2 15.1 %collective-permute-done.20 = bf16[2,64,1536]{2,1,0:T(8,128)(2,1)S(1)} collective-permute-done((bf16[2,64,1536]{2,1,0:T(8,128)(2,1)S(1)}, bf16[2,64,1536]{2,1,0:T(8,128)(2,1)S(1)}, u32[]{:S(2)}, u32[]{:S(2)}) %collective-permute-start.20) | collective-permute-done | bytes 393248 | tf_op jit(solution)/shard_map/ppermute | solution.py:145
  280.5 5.8 collective-permute-done.21
  296.2 17.8 %collective-permute-done.42.refs_7_ = bf16[16,48,1152]{2,1,0:T(8,128)(2,1)} collective-permute-done((bf16[16,48,1152]{2,1,0:T(8,128)(2,1)}, bf16[16,48,1152]{2,1,0:T(8,128)(2,1)}, u32[]{:S(2)}, u32[]{:S(2)}) %collective-permute-start.42) | collective-permute-done | bytes 1769504 | tf_op jit(solution)/shard_map/ppermute | solution.py:73
  317.5 7.6 %collective-permute-done.32.refs_3_ = bf16[16,48,1152]{2,1,0:T(8,128)(2,1)} collective-permute-done((bf16[16,48,1152]{2,1,0:T(8,128)(2,1)}, bf16[16,48,1152]{2,1,0:T(8,128)(2,1)}, u32[]{:S(2)}, u32[]{:S(2)}) %collective-permute-start.32) | collective-permute-done | bytes 1769504 | tf_op jit(solution)/shard_map/ppermute | solution.py:73
  325.0 7.7 %collective-permute-done.27.refs_1_ = bf16[16,48,1152]{2,1,0:T(8,128)(2,1)} collective-permute-done((bf16[16,48,1152]{2,1,0:T(8,128)(2,1)}, bf16[16,48,1152]{2,1,0:T(8,128)(2,1)}, u32[]{:S(2)}, u32[]{:S(2)}) %collective-permute-start.27) | collective-permute-done | bytes 1769504 | tf_op jit(solution)/shard_map/ppermute | solution.py:73
  332.7 27.4 %run_experts.1 = (f32[2,128,1664]{2,1,0:T(8,128)}, bf16[2,128,1664]{2,1,0:T(8,128)(2,1)}, f32[2,128,1536]{2,1,0:T(8,128)S(1)}, bf16[2,128,1536]{2,1,0:T(8,128)(2...) custom-call(s32[4,32]{1,0:T(4,128)S(1)} %broadcast_xor_fusion.places_ref, s32[1]{0:T(128)} %bitcast.55.ep_ref, ...), custom_call_target="tpu_custom_call" | custom-call | flops 14495514624 | bytes 31457280 | tf_op jit(solution)/shard_map/run_experts/pallas_call | solution.py:514
  382.3 5.6 expert_grads.7
  388.5 8.2 %collective-permute-done.46 = bf16[2,64,1664]{2,1,0:T(8,128)(2,1)S(1)} collective-permute-done((bf16[2,64,1664]{2,1,0:T(8,128)(2,1)S(1)}, bf16[2,64,1664]{2,1,0:T(8,128)(2,1)S(1)}, u32[]{:S(2)}, u32[]{:S(2)}) %collective-permute-start.46) | collective-permute-done | bytes 426016 | tf_op jit(solution)/shard_map/ppermute | solution.py:145
  401.2 5.8 expert_grads.6
  445.3 7.4 %all-to-all-start.4 = ((bf16[32,48,512]{2,1,0:T(8,128)(2,1)}), bf16[32,48,512]{2,1,0:T(8,128)(2,1)}, u32[]{:S(2)}, u32[]{:S(2)}) async-start(bf16[32,48,512]{2,1,0:T(8,128)(2,1)} %bitcast.331), calls=%async_computation.4 | async-start | bytes 3145728 | tf_op jit(solution)/shard_map/all_to_all | solution.py:46
  462.2 45.1 %attend_back.1 = (bf16[4,3,64,256]{3,2,1,0:T(8,128)(2,1)S(1)}, bf16[32,256,128]{2,1,0:T(8,128)(2,1)}) custom-call(s32[4]{0:T(128)S(1)} %add_add_fusion.1.blocks_ref, bf16[4,3,64,256]{3,2,1,0:T(8,128)(2,1)S(1)} %copy-done.22, bf16[4,3,64,256]{3,2,1,0:T(8,128)(2,1)S(1)} %pad_maximum_fusion.19.do_ref, bf16[32,256,128]{2,1,0:T(8,128)(2,1)S(1)} %copy-done.7, ...), custom_call_target="tpu_custom_call" | custom-call | flops 16609443840 | bytes 6291456 | tf_op jit(solution)/shard_map/attend_back/pallas_call | solution.py:599
  512.4 4.9 collective-permute-start.54
  526.3 12.6 %collective-permute-done.75 = bf16[8,48,1152]{2,1,0:T(8,128)(2,1)S(1)} collective-permute-done((bf16[8,48,1152]{2,1,0:T(8,128)(2,1)S(1)}, bf16[8,48,1152]{2,1,0:T(8,128)(2,1)S(1)}, u32[]{:S(2)}, u32[]{:S(2)}) %collective-permute-start.75) | collective-permute-done | bytes 884768 | tf_op jit(solution)/shard_map/ppermute | solution.py:73
  554.7 4.8 collective-permute-start.72
  562.0 8.5 %all-to-all-start.2 = ((bf16[32,256,128]{2,1,0:T(8,128)(2,1)}), bf16[32,256,128]{2,1,0:T(8,128)(2,1)S(1)}, u32[]{:S(2)}, u32[]{:S(2)}) async-start(bf16[32,256,128]{2,1,0:T(8,128)(2,1)} %get-tuple-element.37), calls=%async_computation.2 | async-start | bytes 4194304 | tf_op jit(solution)/shard_map/all_to_all | solution.py:876
  580.4 11.3 %collective-permute-start.68 = (bf16[1,48,1152]{2,1,0:T(8,128)(2,1)S(1)}, bf16[1,48,1152]{2,1,0:T(8,128)(2,1)S(1)}, u32[]{:S(2)}, u32[]{:S(2)}) collective-permute-start(bf16[1,48,1152]{2,1,0:T(8,128)(2,1)S(1)} %slice.741), channel_id=1, source_target_pairs={{0,4},{4,0},{8,12},{12,8},{16,20},{20,16},{24,28},{28,24},{32,36},... | collective-permute-start | bytes 331784 | tf_op jit(solution)/shard_map/ppermute | solution.py:73
  604.0 8.0 %all-to-all-start.3 = ((bf16[32,48,640]{2,1,0:T(8,128)(2,1)}), bf16[32,48,640]{2,1,0:T(8,128)(2,1)}, u32[]{:S(2)}, u32[]{:S(2)}) async-start(bf16[32,48,640]{2,1,0:T(8,128)(2,1)} %bitcast.139), calls=%async_computation.3 | async-start | bytes 3932160 | tf_op jit(solution)/shard_map/all_to_all | solution.py:46
  617.8 26.2 %collective-permute-done.56 = bf16[2,64,1536]{2,1,0:T(8,128)(2,1)S(1)} collective-permute-done((bf16[2,64,1536]{2,1,0:T(8,128)(2,1)S(1)}, bf16[2,64,1536]{2,1,0:T(8,128)(2,1)S(1)}, u32[]{:S(2)}, u32[]{:S(2)}) %collective-permute-start.56) | collective-permute-done | bytes 393248 | tf_op jit(solution)/shard_map/ppermute | solution.py:145
  (770 shorter events, 317.5 us)
Async XLA Ops:
  6.5 39.0 %collective-permute-start = (bf16[2,64,1536]{2,1,0:T(8,128)(2,1)}, bf16[2,64,1536]{2,1,0:T(8,128)(2,1)S(1)}, u32[]{:S(2)}, u32[]{:S(2)}) collective-permute-start(bf16[2,64,1536]{2,1,0:T(8,128)(2,1)} %param.24), channel_id=1, source_target_pairs={{0,2},{1,3},{2,0},{3,1},{4,6},{5,7},{6,4},{7,5},{8,10},{9,11},{10,... | collective-permute-start | bytes 1179656 | tf_op jit(solution)/shard_map/ppermute | solution.py:145
  9.5 37.3 %collective-permute-start.2 = (bf16[2,64,128]{1,0,2:T(2,128)(2,1)S(1)}, bf16[2,64,128]{1,0,2:T(2,128)(2,1)}, u32[]{:S(2)}, u32[]{:S(2)}) collective-permute-start(bf16[2,64,128]{1,0,2:T(2,128)(2,1)S(1)} %pad_convert_fusion), channel_id=1, source_target_pairs={{0,2},{1,3},{2,0},{3,1},{4,6},{5,7},{6,4},{7,5},{8,10},{9,11},{10,... | collective-permute-start | bytes 98312 | tf_op jit(solution)/shard_map/ppermute | solution.py:145
  34.4 41.2 %all-to-all-start = ((bf16[32,48,768]{2,1,0:T(8,128)(2,1)}), bf16[32,48,768]{2,1,0:T(8,128)(2,1)}, u32[]{:S(2)}, u32[]{:S(2)}) async-start(bf16[32,48,768]{2,1,0:T(8,128)(2,1)} %broadcast_in_dim.28), calls=%async_computation | async-start | bytes 4718592 | tf_op jit(solution)/shard_map/all_to_all | solution.py:42
  48.4 241.4 %collective-permute-start.3 = (bf16[2,128,128]{1,0,2:T(2,128)(2,1)}, bf16[2,128,128]{1,0,2:T(2,128)(2,1)}, u32[]{:S(2)}, u32[]{:S(2)}) collective-permute-start(bf16[2,128,128]{1,0,2:T(2,128)(2,1)} %pad_maximum_fusion.39), channel_id=1, source_target_pairs={{0,1},{1,0},{2,3},{3,2},{4,5},{5,4},{6,7},{7,6},{8,9},{9,8},{10,11... | collective-permute-start | bytes 196616 | tf_op jit(solution)/shard_map/ppermute | solution.py:145
  86.3 62.5 %collective-permute-start.38 = (bf16[1,48,1152]{2,1,0:T(8,128)(2,1)S(1)}, bf16[1,48,1152]{2,1,0:T(8,128)(2,1)S(1)}, u32[]{:S(2)}, u32[]{:S(2)}) collective-permute-start(bf16[1,48,1152]{2,1,0:T(8,128)(2,1)S(1)} %get-tuple-element.67), channel_id=1, source_target_pairs={{0,12},{4,8},{8,4},{12,0},{16,28},{20,24},{24,20},{28,16},{32,44},... | collective-permute-start | bytes 331784 | tf_op jit(solution)/shard_map/ppermute | solution.py:73
  87.4 49.6 %collective-permute-start.14 = (bf16[1,1,1,48,384]{4,3,2,1,0:T(8,128)(2,1)}, bf16[1,1,1,48,384]{4,3,2,1,0:T(8,128)(2,1)}, u32[]{:S(2)}, u32[]{:S(2)}) collective-permute-start(bf16[1,1,1,48,384]{4,3,2,1,0:T(8,128)(2,1)} %get-tuple-element.165), channel_id=1, source_target_pairs={{0,96},{4,100},{8,104},{12,108},{16,112},{20,116},{24,120},{28,124... | collective-permute-start | bytes 110600 | tf_op jit(solution)/shard_map/ppermute | solution.py:73
  96.0 90.8 %all-to-all-start.1 = ((bf16[32,256,128]{2,1,0:T(8,128)(2,1)}), bf16[32,256,128]{2,1,0:T(8,128)(2,1)S(1)}, u32[]{:S(2)}, u32[]{:S(2)}) async-start(bf16[32,256,128]{2,1,0:T(8,128)(2,1)} %bitcast.323), calls=%async_computation.1 | async-start | bytes 4194304 | tf_op jit(solution)/shard_map/all_to_all | solution.py:773
  107.0 35.4 %collective-permute-start.8 = (bf16[3,64,256]{2,1,0:T(8,128)(2,1)}, bf16[3,64,256]{2,1,0:T(8,128)(2,1)S(1)}, u32[]{:S(2)}, u32[]{:S(2)}) collective-permute-start(bf16[3,64,256]{2,1,0:T(8,128)(2,1)} %get-tuple-element.114), channel_id=1, source_target_pairs={{0,60},{4,56},{8,52},{12,48},{16,44},{20,40},{24,36},{28,32},{32,2... | collective-permute-start | bytes 294920 | tf_op jit(solution)/shard_map/ppermute | solution.py:186
  108.5 34.3 %collective-permute-start.9 = (bf16[3,64,256]{2,1,0:T(8,128)(2,1)}, bf16[3,64,256]{2,1,0:T(8,128)(2,1)S(1)}, u32[]{:S(2)}, u32[]{:S(2)}) collective-permute-start(bf16[3,64,256]{2,1,0:T(8,128)(2,1)} %get-tuple-element.113), channel_id=1, source_target_pairs={{0,64},{4,68},{8,72},{12,76},{16,80},{20,84},{24,88},{28,92},{32,9... | collective-permute-start | bytes 294920 | tf_op jit(solution)/shard_map/ppermute | solution.py:186
  174.8 69.5 %collective-permute-start.30 = (bf16[4,48,1152]{2,1,0:T(8,128)(2,1)}, bf16[4,48,1152]{2,1,0:T(8,128)(2,1)}, u32[]{:S(2)}, u32[]{:S(2)}) collective-permute-start(bf16[4,48,1152]{2,1,0:T(8,128)(2,1)} %pad_maximum_fusion.13), channel_id=1, source_target_pairs={{0,12},{4,8},{8,4},{12,0},{16,28},{20,24},{24,20},{28,16},{32,44},... | collective-permute-start | bytes 1327112 | tf_op jit(solution)/shard_map/ppermute | solution.py:73
  179.8 51.9 %collective-permute-start.18 = (bf16[4,2,2,48,384]{4,3,2,1,0:T(8,128)(2,1)}, bf16[4,2,2,48,384]{4,3,2,1,0:T(8,128)(2,1)}, u32[]{:S(2)}, u32[]{:S(2)}) collective-permute-start(bf16[4,2,2,48,384]{4,3,2,1,0:T(8,128)(2,1)} %pad_maximum_fusion.11), channel_id=1, source_target_pairs={{0,12},{4,8},{8,4},{12,0},{16,28},{20,24},{24,20},{28,16},{32,44},... | collective-permute-start | bytes 1769480 | tf_op jit(solution)/shard_map/ppermute | solution.py:73
  246.9 31.2 %collective-permute-start.31 = (bf16[8,48,1152]{2,1,0:T(8,128)(2,1)S(1)}, bf16[8,48,1152]{2,1,0:T(8,128)(2,1)S(1)}, u32[]{:S(2)}, u32[]{:S(2)}) collective-permute-start(bf16[8,48,1152]{2,1,0:T(8,128)(2,1)S(1)} %pad_maximum_fusion.4), channel_id=1, source_target_pairs={{0,96},{4,100},{8,104},{12,108},{16,112},{20,116},{24,120},{28,124... | collective-permute-start | bytes 2654216 | tf_op jit(solution)/shard_map/ppermute | solution.py:73
  254.6 34.2 %collective-permute-start.26 = (bf16[8,48,1152]{2,1,0:T(8,128)(2,1)S(1)}, bf16[8,48,1152]{2,1,0:T(8,128)(2,1)S(1)}, u32[]{:S(2)}, u32[]{:S(2)}) collective-permute-start(bf16[8,48,1152]{2,1,0:T(8,128)(2,1)S(1)} %pad_maximum_fusion.3), channel_id=1, source_target_pairs={{0,12},{4,8},{8,4},{12,0},{16,28},{20,24},{24,20},{28,16},{32,44},... | collective-permute-start | bytes 2654216 | tf_op jit(solution)/shard_map/ppermute | solution.py:73
  274.4 39.7 %collective-permute-start.42 = (bf16[16,48,1152]{2,1,0:T(8,128)(2,1)}, bf16[16,48,1152]{2,1,0:T(8,128)(2,1)}, u32[]{:S(2)}, u32[]{:S(2)}) collective-permute-start(bf16[16,48,1152]{2,1,0:T(8,128)(2,1)} %constant_dynamic-update-slice_fusion.18.refs_6_), channel_id=1, source_target_pairs={{0,32},{4,36},{8,40},{12,44},{16,48},{20,52},{24,56},{28,60},{32,0... | collective-permute-start | bytes 5308424 | tf_op jit(solution)/shard_map/ppermute | solution.py:73
  278.1 39.4 %collective-permute-start.37 = (bf16[16,48,1152]{2,1,0:T(8,128)(2,1)}, bf16[16,48,1152]{2,1,0:T(8,128)(2,1)}, u32[]{:S(2)}, u32[]{:S(2)}) collective-permute-start(bf16[16,48,1152]{2,1,0:T(8,128)(2,1)} %constant_dynamic-update-slice_fusion.13.refs_4_), channel_id=1, source_target_pairs={{0,4},{4,0},{8,12},{12,8},{16,20},{20,16},{24,28},{28,24},{32,36},... | collective-permute-start | bytes 5308424 | tf_op jit(solution)/shard_map/ppermute | solution.py:73
  286.3 38.7 %collective-permute-start.32 = (bf16[16,48,1152]{2,1,0:T(8,128)(2,1)}, bf16[16,48,1152]{2,1,0:T(8,128)(2,1)}, u32[]{:S(2)}, u32[]{:S(2)}) collective-permute-start(bf16[16,48,1152]{2,1,0:T(8,128)(2,1)} %constant_dynamic-update-slice_fusion.8.refs_2_), channel_id=1, source_target_pairs={{0,16},{4,20},{8,24},{12,28},{16,0},{20,4},{24,8},{28,12},{32,48},... | collective-permute-start | bytes 5308424 | tf_op jit(solution)/shard_map/ppermute | solution.py:73
  289.8 42.9 %collective-permute-start.27 = (bf16[16,48,1152]{2,1,0:T(8,128)(2,1)}, bf16[16,48,1152]{2,1,0:T(8,128)(2,1)}, u32[]{:S(2)}, u32[]{:S(2)}) collective-permute-start(bf16[16,48,1152]{2,1,0:T(8,128)(2,1)} %constant_dynamic-update-slice_fusion.3.refs_0_), channel_id=1, source_target_pairs={{0,96},{4,100},{8,104},{12,108},{16,112},{20,116},{24,120},{28,124... | collective-permute-start | bytes 5308424 | tf_op jit(solution)/shard_map/ppermute | solution.py:73
  387.9 120.6 %collective-permute-start.74 = (bf16[16,48,1152]{2,1,0:T(8,128)(2,1)}, bf16[16,48,1152]{2,1,0:T(8,128)(2,1)}, u32[]{:S(2)}, u32[]{:S(2)}) collective-permute-start(bf16[16,48,1152]{2,1,0:T(8,128)(2,1)} %get-tuple-element.47), channel_id=1, source_target_pairs={{0,32},{4,36},{8,40},{12,44},{16,48},{20,52},{24,56},{28,60},{32,0... | collective-permute-start | bytes 5308424 | tf_op jit(solution)/shard_map/ppermute | solution.py:73
  408.2 104.1 %collective-permute-start.69 = (bf16[16,48,1152]{2,1,0:T(8,128)(2,1)}, bf16[16,48,1152]{2,1,0:T(8,128)(2,1)}, u32[]{:S(2)}, u32[]{:S(2)}) collective-permute-start(bf16[16,48,1152]{2,1,0:T(8,128)(2,1)} %get-tuple-element.45), channel_id=1, source_target_pairs={{0,4},{4,0},{8,12},{12,8},{16,20},{20,16},{24,28},{28,24},{32,36},... | collective-permute-start | bytes 5308424 | tf_op jit(solution)/shard_map/ppermute | solution.py:73
  445.3 116.7 %all-to-all-start.4 = ((bf16[32,48,512]{2,1,0:T(8,128)(2,1)}), bf16[32,48,512]{2,1,0:T(8,128)(2,1)}, u32[]{:S(2)}, u32[]{:S(2)}) async-start(bf16[32,48,512]{2,1,0:T(8,128)(2,1)} %bitcast.331), calls=%async_computation.4 | async-start | bytes 3145728 | tf_op jit(solution)/shard_map/all_to_all | solution.py:46
  453.3 66.0 %collective-permute-start.59 = (bf16[16,48,1152]{2,1,0:T(8,128)(2,1)}, bf16[16,48,1152]{2,1,0:T(8,128)(2,1)S(1)}, u32[]{:S(2)}, u32[]{:S(2)}) collective-permute-start(bf16[16,48,1152]{2,1,0:T(8,128)(2,1)} %copy-done.30), channel_id=1, source_target_pairs={{0,96},{4,100},{8,104},{12,108},{16,112},{20,116},{24,120},{28,124... | collective-permute-start | bytes 5308424 | tf_op jit(solution)/shard_map/ppermute | solution.py:73
  456.1 65.1 %collective-permute-start.64 = (bf16[16,48,1152]{2,1,0:T(8,128)(2,1)}, bf16[16,48,1152]{2,1,0:T(8,128)(2,1)S(1)}, u32[]{:S(2)}, u32[]{:S(2)}) collective-permute-start(bf16[16,48,1152]{2,1,0:T(8,128)(2,1)} %copy-done.29), channel_id=1, source_target_pairs={{0,16},{4,20},{8,24},{12,28},{16,0},{20,4},{24,8},{28,12},{32,48},... | collective-permute-start | bytes 5308424 | tf_op jit(solution)/shard_map/ppermute | solution.py:73
  562.0 32.5 %all-to-all-start.2 = ((bf16[32,256,128]{2,1,0:T(8,128)(2,1)}), bf16[32,256,128]{2,1,0:T(8,128)(2,1)S(1)}, u32[]{:S(2)}, u32[]{:S(2)}) async-start(bf16[32,256,128]{2,1,0:T(8,128)(2,1)} %get-tuple-element.37), calls=%async_computation.2 | async-start | bytes 4194304 | tf_op jit(solution)/shard_map/all_to_all | solution.py:876
  604.0 41.6 %all-to-all-start.3 = ((bf16[32,48,640]{2,1,0:T(8,128)(2,1)}), bf16[32,48,640]{2,1,0:T(8,128)(2,1)}, u32[]{:S(2)}, u32[]{:S(2)}) async-start(bf16[32,48,640]{2,1,0:T(8,128)(2,1)} %bitcast.139), calls=%async_computation.3 | async-start | bytes 3932160 | tf_op jit(solution)/shard_map/all_to_all | solution.py:46
  (214 other events, 2493.0 us)

commit v2 on v1

--- a/solution.py
+++ b/solution.py
@@ -127,18 +127,17 @@
     return part.reshape(-1, part.shape[-1])
 
 
-def sum_links(pairs):
-    for step in reversed(range(len(LINKS))):
+def sum_links(pairs, steps):
+    for step in steps:
         sums = [
             kept.astype(F32) + across_link(sent, link_of(step, at)).astype(F32)
             for at, (kept, sent) in enumerate(pairs)
         ]
-        pairs = []
-        for total in sums:
-            half = total.shape[0] // 2
-            total = total.astype(BF16) if step else total
-            pairs.append((total[:half], total[half:]))
-    return [total[0] for total in sums]
+        if not step:
+            return [total[0] for total in sums]
+        sums = [total.astype(BF16) for total in sums]
+        pairs = [(total[: len(total) // 2], total[len(total) // 2 :]) for total in sums]
+    return pairs
 
 
 def across_ep(value, distance):
@@ -288,11 +287,35 @@
             )
             return carry
 
+        def several(turn, carry):
+            first = 1 + 4 * turn
+            parts = [kv_ref[first + at] for at in range(4)]
+            scores = [dot(part, q_wide[...]) for part in parts]
+            highest = top[...]
+            for score in scores:
+                highest = jnp.maximum(highest, jnp.max(score, axis=0, keepdims=True))
+            new_top = jnp.where(covered, highest, top[...])
+            scale_by = jnp.where(covered, new_top, -MASKED)
+            weights = [jnp.exp(score - scale_by) for score in scores]
+            shrink = jnp.exp(top[...] - new_top)
+            top[...] = new_top
+            total[...] = total[...] * shrink + sum(
+                jnp.sum(weight, axis=0, keepdims=True) for weight in weights
+            )
+            added = sum(
+                dot_rows(part, weight.astype(BF16))[HEAD_DIM:]
+                for part, weight in zip(parts, weights)
+            )
+            acc[...] = acc[...] * shrink + added
+            return carry
+
         @pl.when(query_block > 0)
         def _():
             edge(0, COMBOS)
 
-        lax.fori_loop(1, query_block, inner, 0)
+        turns = jnp.maximum(query_block - 1, 0) // 4
+        lax.fori_loop(0, turns, several, 0)
+        lax.fori_loop(1 + 4 * turns, query_block, inner, 0)
         edge(query_block, side)
         lse_ref[side] = top[...] + jnp.log(total[...])
         result = acc[...] / total[...]
@@ -369,11 +392,31 @@
             add(block, dot(kv_ref[block], q_wide[...]), covered_lse)
             return carry
 
+        def several(turn, carry):
+            first = 1 + 4 * turn
+            parts = [kv_ref[first + at] for at in range(4)]
+            scores = [dot(part, q_wide[...]) for part in parts]
+            grads = [dot(part, do_wide[...]) for part in parts]
+            weights = [jnp.exp(score - covered_lse) for score in scores]
+            grads = [
+                (weight * (grad - delta)).astype(BF16) for weight, grad in zip(weights, grads)
+            ]
+            for at in range(4):
+                dkv_acc[first + at] += dot(grads[at], q_tall[...]) + dot(
+                    weights[at].astype(BF16), do_tall[...]
+                )
+            dq_acc[...] += sum(
+                dot_rows(part, grad)[:HEAD_DIM] for part, grad in zip(parts, grads)
+            )
+            return carry
+
         @pl.when(query_block > 0)
         def _():
             edge(0, COMBOS)
 
-        lax.fori_loop(1, query_block, inner, 0)
+        turns = jnp.maximum(query_block - 1, 0) // 4
+        lax.fori_loop(0, turns, several, 0)
+        lax.fori_loop(1 + 4 * turns, query_block, inner, 0)
         edge(query_block, side)
         for head in range(GROUP):
             at = slice(head * BLOCK, (head + 1) * BLOCK)
@@ -815,7 +858,8 @@
                 q, grad_places[q], tokens_all, cotangent_all, grad_pre, gated_hidden, rows_weight
             )
             for q in range(4)
-        ]
+        ],
+        (4,),
     )
     outputs = (residual + finish_sum(out_kept, across_ep(out_sent, 1))).astype(BF16)
 
@@ -831,6 +875,13 @@
     )
     grad_router = jnp.einsum("btd,bte->de", tokens, grad_logits, preferred_element_type=F32)
     grad_gain_two = jnp.sum(grad_tokens * normal_two, axis=(0, 1))
+    small_grads = jnp.concatenate([grad_gain_two[:, None], grad_router], axis=1)
+    small_high = lax.reduce_precision(small_grads, 8, 7)
+    small_count = small_grads.shape[1]
+    small_message = (
+        jnp.pad(small_high, ((0, 0), (0, 128 - small_count)))
+        + jnp.pad(small_grads - small_high, ((0, 0), (small_count, 128 - 2 * small_count)))
+    ).astype(BF16)
     scaled = grad_tokens * gain_two
     grad_residual = cotangent.astype(F32) + scale_two * (
         scaled - normal_two * jnp.mean(scaled * normal_two, axis=-1, keepdims=True)
@@ -841,27 +892,11 @@
     ).astype(BF16)
     grad_mixed = to_attention(grad_mixed)
 
-    small_grads = jnp.concatenate([grad_gain_two[:, None], grad_router], axis=1)
-    small_high = lax.reduce_precision(small_grads, 8, 7)
-    small_count = small_grads.shape[1]
-    grad_out = jnp.einsum("td,ht->dh", grad_attn, mixed, preferred_element_type=F32)
-    grad_out = jnp.concatenate(
-        [
-            grad_out.astype(BF16),
-            small_high.astype(BF16),
-            (small_grads - small_high).astype(BF16),
-            jnp.zeros((width, 128 - 2 * small_count), BF16),
-        ],
-        axis=1,
-    )
-    blocks = after(blocks, grad_out, outputs)
-    grad_out = sum_ctx(grad_out.reshape(ctx_count, rows_weight, width_query + 128))
-    small_grads = (
-        grad_out[:, width_query : width_query + small_count]
-        + grad_out[:, width_query + small_count : width_query + 2 * small_count]
-    )
-    grad_out = grad_out[:, :width_query].T
-
+    grad_out = jnp.einsum(
+        "td,ht->dh", grad_attn, mixed, preferred_element_type=F32
+    ).astype(BF16)
+    side_message = jnp.concatenate([grad_out, small_message], axis=1)
+    blocks = after(blocks, outputs, side_message[:, width_query:])
     grad_queries, grad_keys_values = attend_back(
         blocks,
         queries,
@@ -873,7 +908,10 @@
         cosines,
         sines,
     )
-    received = lax.all_to_all(grad_keys_values, "ctx", 0, 0, tiled=True).astype(F32)
+    received = lax.all_to_all(grad_keys_values, "ctx", 0, 0, tiled=True)
+    grad_parts = [(after(kept, received), sent) for kept, sent in grad_parts]
+    grad_parts = sum_links(grad_parts, (3, 2, 1, 0))
+    received = received.astype(F32)
     received = jnp.sum(
         received.reshape(COMBOS, ctx_count // COMBOS, BLOCK, 2 * HEAD_DIM), axis=1
     ).transpose(0, 2, 1)
@@ -888,6 +926,10 @@
     grad_partial = dot_rows(
         jnp.concatenate([grad_query, grad_kv]), joined.T
     )
+    grad_joined = jnp.concatenate([grad_query, grad_kv])
+    grad_joined = jnp.einsum("td,ct->dc", normed, grad_joined, preferred_element_type=F32)
+    last_message = jnp.concatenate([grad_joined.astype(BF16), side_message], axis=1)
+    grad_partial = after(grad_partial, last_message)
     grad_normed = sum_ep(grad_partial.reshape(MB, BLOCK, width), 1)
     values = inputs.astype(F32)
     scale_own = rms_scale(values)
@@ -899,10 +941,13 @@
         * (scaled - normal_own * jnp.mean(scaled * normal_own, axis=-1, keepdims=True))
     ).astype(BF16)
 
-    grad_joined = jnp.concatenate([grad_query, grad_kv])
-    grad_joined = jnp.einsum("td,ct->dc", normed, grad_joined, preferred_element_type=F32)
-    grad_joined = sum_ctx(
-        grad_joined.astype(BF16).reshape(ctx_count, rows_weight, width_joined)
+    last_sums = sum_ctx(last_message.reshape(ctx_count, rows_weight, last_message.shape[1]))
+    grad_joined = last_sums[:, :width_joined]
+    small_at = width_joined + width_query
+    grad_out = last_sums[:, width_joined:small_at].T
+    small_grads = (
+        last_sums[:, small_at : small_at + small_count]
+        + last_sums[:, small_at + small_count : small_at + 2 * small_count]
     )
     grad_w_query = grad_joined[:, :width_query]
     grad_w_kv = grad_joined[:, width_query:]

time: 673 us -> 646 us (0.960)
  starting transfers between devices: 167 us -> 144 us
  waiting for transfers between devices: 147 us -> 163 us
  Pallas kernels: 133 us -> 120 us
  local copies, waits for them, and re-layouts: 105 us -> 96.3 us
    ppermute x45, waiting for transfers between devices: 61.1 us -> 83.9 us  [across_link(): return lax.ppermute(value, 'ctx', [(i, partner(i)) for i in range(size)])]
    ppermute x22, waiting for transfers between devices: 58.7 us -> 40.4 us  [across_ep(): return lax.ppermute(value, 'ep', [(i, i ^ distance) for i in range(4)])]
    ppermute x12, starting transfers between devices: 42.2 us -> 31.6 us  [across_quad(): lax.ppermute(value, 'ctx', [(i, quad_member(i, size, distance)) for i in...]
    ppermute x12, waiting for transfers between devices: 5.48 us -> 15.5 us  [across_quad(): lax.ppermute(value, 'ctx', [(i, quad_member(i, size, distance)) for i in...]
    pallas_call x1, Pallas kernels: 41 us -> 31 us  [attend(): pl.pallas_call(forward_kernel, out_shape=(jax.ShapeDtypeStruct(HEADS_SHAP...]
    convert_element_type x18 -> x17, other arithmetic: 10.3 us -> 18.8 us  [the longest x16 18.5 us: sum_links(): sums = [total.astype(BF16) for total in sums]]
    all_to_all x2 -> x1, starting transfers between devices: 15.4 us -> 7.2 us  [sum_ctx(): lax.all_to_all(parts, 'ctx', 0, 0, tiled=True).astype(F32)]
    unnamed x340 -> x352, local copies, waits for them, and re-layouts: 39.8 us -> 33.1 us
  transfers between devices with their start and end apart: 84 -> 83, of which waited for: 22 -> 20; matrix products, arithmetic and copies ran while one was open for 24% -> 26% of each run, Pallas kernels for 16% -> 15%
where the time goes in v2:
time: 646 us; the launch traced here: 635 us
  waiting for transfers between devices  163 us (25%)
  starting transfers between devices  144 us (22%)
  Pallas kernels  120 us (19%)
  local copies, waits for them, and re-layouts  96.3 us (15%)
  other arithmetic  79.1 us (12%)
  between operations  19.9 us (3%)
  matrix products  12.4 us (2%)
    ppermute x45, waiting for transfers between devices, across_link(): return lax.ppermute(value, 'ctx', [(i, partner(i)) for i in range(size)])  83.9 us
    ppermute x45, starting transfers between devices, across_link(): return lax.ppermute(value, 'ctx', [(i, partner(i)) for i in range(size)])  62.2 us
    ppermute x22, waiting for transfers between devices, across_ep(): return lax.ppermute(value, 'ep', [(i, i ^ distance) for i in range(4)])  40.4 us
    pallas_call x1, Pallas kernels, attend_back(): pl.pallas_call(backward_kernel, out_shape=(jax.ShapeDtypeStruct(HEADS_SHA...  39.2 us
    unnamed x352, local copies, waits for them, and re-layouts  33.1 us
    ppermute x12, starting transfers between devices, across_quad(): lax.ppermute(value, 'ctx', [(i, quad_member(i, size, distance)) for i in...  31.6 us
    pallas_call x1, Pallas kernels, attend(): pl.pallas_call(forward_kernel, out_shape=(jax.ShapeDtypeStruct(HEADS_SHAP...  31 us
    pallas_call x1, Pallas kernels, run_experts(): pl.pallas_call(experts_kernel, out_shape=(jax.ShapeDtypeStruct((*kept_row...  27.4 us
  transfers between devices with their start and end apart: 83, of which 20 were waited for; matrix products, arithmetic and copies ran while one was open for 26% of the time, Pallas kernels for 15%

profile of v2, /device:TPU:26, one launch (start us, length us, event | category | flops | bytes accessed | tf_op | source)
XLA Modules:
  0.0 634.7 jit_solution(8138971261668422147)
XLA Ops:
  34.4 9.4 %all-to-all-start = ((bf16[32,48,768]{2,1,0:T(8,128)(2,1)}), bf16[32,48,768]{2,1,0:T(8,128)(2,1)}, u32[]{:S(2)}, u32[]{:S(2)}) async-start(bf16[32,48,768]{2,1,0:T(8,128)(2,1)} %broadcast_in_dim.26), calls=%async_computation | async-start | bytes 4718592 | tf_op jit(solution)/shard_map/all_to_all | solution.py:42
  52.7 22.8 %all-to-all-done = bf16[32,48,768]{2,1,0:T(8,128)(2,1)} async-done(((bf16[32,48,768]{2,1,0:T(8,128)(2,1)}), bf16[32,48,768]{2,1,0:T(8,128)(2,1)}, u32[]{:S(2)}, u32[]{:S(2)}) %all-to-all-start) | async-done | bytes 2359328 | tf_op jit(solution)/shard_map/all_to_all | solution.py:42
  96.5 7.2 %all-to-all-start.1 = ((bf16[32,256,128]{2,1,0:T(8,128)(2,1)}), bf16[32,256,128]{2,1,0:T(8,128)(2,1)S(1)}, u32[]{:S(2)}, u32[]{:S(2)}) async-start(bf16[32,256,128]{2,1,0:T(8,128)(2,1)} %bitcast.323), calls=%async_computation.1 | async-start | bytes 4194304 | tf_op jit(solution)/shard_map/all_to_all | solution.py:816
  177.9 31.0 %attend.1 = (f32[4,3,64,256]{3,2,1,0:T(8,128)S(1)}, f32[4,1,768]{2,1,0:T(1,128)S(1)}) custom-call(s32[4]{0:T(128)S(1)} %add_add_fusion.2.blocks_ref, bf16[4,3,64,256]{3,2,1,0:T(8,128)(2,1)S(1)} %pad_maximum_fusion.17.q_ref, bf16[32,256,128]{2,1,0:T(8,128)(2,1)S(1)} %all-to-all-done.1.kv_ref, f32[4,1,768]{2,1,0:T(1,128)S(1)} %copy.289.seg_row_ref, ...), custom_call_target="tpu_custom_call" | custom-call | flops 6643777536 | bytes 4194304 | tf_op jit(solution)/shard_map/attend/pallas_call | solution.py:616
  211.6 5.4 collective-permute-start.13
  241.1 15.6 %collective-permute-done.20 = bf16[2,64,1536]{2,1,0:T(8,128)(2,1)S(1)} collective-permute-done((bf16[2,64,1536]{2,1,0:T(8,128)(2,1)S(1)}, bf16[2,64,1536]{2,1,0:T(8,128)(2,1)S(1)}, u32[]{:S(2)}, u32[]{:S(2)}) %collective-permute-start.20) | collective-permute-done | bytes 393248 | tf_op jit(solution)/shard_map/ppermute | solution.py:144
  262.5 6.2 collective-permute-done.21
  270.7 11.0 %collective-permute-start.27 = (bf16[16,48,1152]{2,1,0:T(8,128)(2,1)}, bf16[16,48,1152]{2,1,0:T(8,128)(2,1)}, u32[]{:S(2)}, u32[]{:S(2)}) collective-permute-start(bf16[16,48,1152]{2,1,0:T(8,128)(2,1)} %constant_dynamic-update-slice_fusion.3.refs_0_), channel_id=1, source_target_pairs={{0,96},{4,100},{8,104},{12,108},{16,112},{20,116},{24,120},{28,124... | collective-permute-start | bytes 5308424 | tf_op jit(solution)/shard_map/ppermute | solution.py:73
  284.3 12.0 %collective-permute-done.42.refs_7_ = bf16[16,48,1152]{2,1,0:T(8,128)(2,1)} collective-permute-done((bf16[16,48,1152]{2,1,0:T(8,128)(2,1)}, bf16[16,48,1152]{2,1,0:T(8,128)(2,1)}, u32[]{:S(2)}, u32[]{:S(2)}) %collective-permute-start.42) | collective-permute-done | bytes 1769504 | tf_op jit(solution)/shard_map/ppermute | solution.py:73
  299.8 7.6 %collective-permute-done.32.refs_3_ = bf16[16,48,1152]{2,1,0:T(8,128)(2,1)} collective-permute-done((bf16[16,48,1152]{2,1,0:T(8,128)(2,1)}, bf16[16,48,1152]{2,1,0:T(8,128)(2,1)}, u32[]{:S(2)}, u32[]{:S(2)}) %collective-permute-start.32) | collective-permute-done | bytes 1769504 | tf_op jit(solution)/shard_map/ppermute | solution.py:73
  307.4 14.4 %collective-permute-done.27.refs_1_ = bf16[16,48,1152]{2,1,0:T(8,128)(2,1)} collective-permute-done((bf16[16,48,1152]{2,1,0:T(8,128)(2,1)}, bf16[16,48,1152]{2,1,0:T(8,128)(2,1)}, u32[]{:S(2)}, u32[]{:S(2)}) %collective-permute-start.27) | collective-permute-done | bytes 1769504 | tf_op jit(solution)/shard_map/ppermute | solution.py:73
  321.8 27.4 %run_experts.1 = (f32[2,128,1664]{2,1,0:T(8,128)}, bf16[2,128,1664]{2,1,0:T(8,128)(2,1)}, f32[2,128,1536]{2,1,0:T(8,128)S(1)}, bf16[2,128,1536]{2,1,0:T(8,128)(2...) custom-call(s32[4,32]{1,0:T(4,128)S(1)} %broadcast_xor_fusion.places_ref, s32[1]{0:T(128)} %bitcast.55.ep_ref, ...), custom_call_target="tpu_custom_call" | custom-call | flops 14495514624 | bytes 31457280 | tf_op jit(solution)/shard_map/run_experts/pallas_call | solution.py:557
  370.8 5.5 expert_grads.7
  377.2 7.9 %collective-permute-done.46 = bf16[2,64,1664]{2,1,0:T(8,128)(2,1)S(1)} collective-permute-done((bf16[2,64,1664]{2,1,0:T(8,128)(2,1)S(1)}, bf16[2,64,1664]{2,1,0:T(8,128)(2,1)S(1)}, u32[]{:S(2)}, u32[]{:S(2)}) %collective-permute-start.46) | collective-permute-done | bytes 426016 | tf_op jit(solution)/shard_map/ppermute | solution.py:144
  390.1 6.0 expert_grads.6
  398.9 5.6 expert_grads.4
  405.7 5.5 expert_grads.5
  436.8 39.2 %attend_back.1 = (bf16[4,3,64,256]{3,2,1,0:T(8,128)(2,1)S(1)}, bf16[32,256,128]{2,1,0:T(8,128)(2,1)}) custom-call(s32[4]{0:T(128)S(1)} %add_add_fusion.1.blocks_ref, bf16[4,3,64,256]{3,2,1,0:T(8,128)(2,1)S(1)} %pad_maximum_fusion.17.q_ref, bf16[4,3,64,256]{3,2,1,0:T(8,128)(2,1)S(1)} %pad_maximum_fusion.20.do_ref, bf16[32,256,128]{2,1,0:T(8,128)(2,1)S(1)} %copy-done.7, ...), custom_call_target="tpu_custom_call" | custom-call | flops 16609443840 | bytes 6291456 | tf_op jit(solution)/shard_map/attend_back/pallas_call | solution.py:642
  476.0 5.8 all-to-all-start.2
  502.6 8.5 %collective-permute-done.52 = bf16[3,64,256]{2,1,0:T(8,128)(2,1)S(1)} collective-permute-done((bf16[3,64,256]{2,1,0:T(8,128)(2,1)S(1)}, bf16[3,64,256]{2,1,0:T(8,128)(2,1)S(1)}, u32[]{:S(2)}, u32[]{:S(2)}) %collective-permute-start.52) | collective-permute-done | bytes 98336 | tf_op jit(solution)/shard_map/ppermute | solution.py:185
  517.6 7.5 %collective-permute-done.75 = bf16[8,48,1152]{2,1,0:T(8,128)(2,1)} collective-permute-done((bf16[8,48,1152]{2,1,0:T(8,128)(2,1)}, bf16[8,48,1152]{2,1,0:T(8,128)(2,1)}, u32[]{:S(2)}, u32[]{:S(2)}) %collective-permute-start.75) | collective-permute-done | bytes 884768 | tf_op jit(solution)/shard_map/ppermute | solution.py:73
  548.9 7.2 %all-to-all-start.3 = ((bf16[32,48,1152]{2,1,0:T(8,128)(2,1)}), bf16[32,48,1152]{2,1,0:T(8,128)(2,1)S(1)}, u32[]{:S(2)}, u32[]{:S(2)}) async-start(bf16[32,48,1152]{2,1,0:T(8,128)(2,1)} %bitcast.322), calls=%async_computation.3 | async-start | bytes 7077888 | tf_op jit(solution)/shard_map/all_to_all | solution.py:46
  570.5 29.2 %collective-permute-done.77 = bf16[2,48,1152]{2,1,0:T(8,128)(2,1)S(1)} collective-permute-done((bf16[2,48,1152]{2,1,0:T(8,128)(2,1)S(1)}, bf16[2,48,1152]{2,1,0:T(8,128)(2,1)S(1)}, u32[]{:S(2)}, u32[]{:S(2)}) %collective-permute-start.77) | collective-permute-done | bytes 221216 | tf_op jit(solution)/shard_map/ppermute | solution.py:73
  616.3 6.2 collective-permute-done.56
  (776 shorter events, 310.7 us)
Async XLA Ops:
  6.5 38.8 %collective-permute-start = (bf16[2,64,1536]{2,1,0:T(8,128)(2,1)}, bf16[2,64,1536]{2,1,0:T(8,128)(2,1)S(1)}, u32[]{:S(2)}, u32[]{:S(2)}) collective-permute-start(bf16[2,64,1536]{2,1,0:T(8,128)(2,1)} %param.24), channel_id=1, source_target_pairs={{0,2},{1,3},{2,0},{3,1},{4,6},{5,7},{6,4},{7,5},{8,10},{9,11},{10,... | collective-permute-start | bytes 1179656 | tf_op jit(solution)/shard_map/ppermute | solution.py:144
  9.5 37.1 %collective-permute-start.2 = (bf16[2,64,128]{1,0,2:T(2,128)(2,1)S(1)}, bf16[2,64,128]{1,0,2:T(2,128)(2,1)S(1)}, u32[]{:S(2)}, u32[]{:S(2)}) collective-permute-start(bf16[2,64,128]{1,0,2:T(2,128)(2,1)S(1)} %pad_convert_fusion), channel_id=1, source_target_pairs={{0,2},{1,3},{2,0},{3,1},{4,6},{5,7},{6,4},{7,5},{8,10},{9,11},{10,... | collective-permute-start | bytes 98312 | tf_op jit(solution)/shard_map/ppermute | solution.py:144
  34.4 41.2 %all-to-all-start = ((bf16[32,48,768]{2,1,0:T(8,128)(2,1)}), bf16[32,48,768]{2,1,0:T(8,128)(2,1)}, u32[]{:S(2)}, u32[]{:S(2)}) async-start(bf16[32,48,768]{2,1,0:T(8,128)(2,1)} %broadcast_in_dim.26), calls=%async_computation | async-start | bytes 4718592 | tf_op jit(solution)/shard_map/all_to_all | solution.py:42
  47.4 223.3 %collective-permute-start.3 = (bf16[2,128,128]{1,0,2:T(2,128)(2,1)}, bf16[2,128,128]{1,0,2:T(2,128)(2,1)}, u32[]{:S(2)}, u32[]{:S(2)}) collective-permute-start(bf16[2,128,128]{1,0,2:T(2,128)(2,1)} %pad_maximum_fusion.40), channel_id=1, source_target_pairs={{0,1},{1,0},{2,3},{3,2},{4,5},{5,4},{6,7},{7,6},{8,9},{9,8},{10,11... | collective-permute-start | bytes 196616 | tf_op jit(solution)/shard_map/ppermute | solution.py:144
  86.2 52.7 %collective-permute-start.38 = (bf16[1,48,1152]{2,1,0:T(8,128)(2,1)S(1)}, bf16[1,48,1152]{2,1,0:T(8,128)(2,1)S(1)}, u32[]{:S(2)}, u32[]{:S(2)}) collective-permute-start(bf16[1,48,1152]{2,1,0:T(8,128)(2,1)S(1)} %get-tuple-element.67), channel_id=1, source_target_pairs={{0,12},{4,8},{8,4},{12,0},{16,28},{20,24},{24,20},{28,16},{32,44},... | collective-permute-start | bytes 331784 | tf_op jit(solution)/shard_map/ppermute | solution.py:73
  87.4 39.9 %collective-permute-start.14 = (bf16[1,1,1,48,384]{4,3,2,1,0:T(8,128)(2,1)}, bf16[1,1,1,48,384]{4,3,2,1,0:T(8,128)(2,1)}, u32[]{:S(2)}, u32[]{:S(2)}) collective-permute-start(bf16[1,1,1,48,384]{4,3,2,1,0:T(8,128)(2,1)} %get-tuple-element.167), channel_id=1, source_target_pairs={{0,96},{4,100},{8,104},{12,108},{16,112},{20,116},{24,120},{28,124... | collective-permute-start | bytes 110600 | tf_op jit(solution)/shard_map/ppermute | solution.py:73
  96.5 80.4 %all-to-all-start.1 = ((bf16[32,256,128]{2,1,0:T(8,128)(2,1)}), bf16[32,256,128]{2,1,0:T(8,128)(2,1)S(1)}, u32[]{:S(2)}, u32[]{:S(2)}) async-start(bf16[32,256,128]{2,1,0:T(8,128)(2,1)} %bitcast.323), calls=%async_computation.1 | async-start | bytes 4194304 | tf_op jit(solution)/shard_map/all_to_all | solution.py:816
  164.9 60.9 %collective-permute-start.30 = (bf16[4,48,1152]{2,1,0:T(8,128)(2,1)}, bf16[4,48,1152]{2,1,0:T(8,128)(2,1)}, u32[]{:S(2)}, u32[]{:S(2)}) collective-permute-start(bf16[4,48,1152]{2,1,0:T(8,128)(2,1)} %pad_maximum_fusion.14), channel_id=1, source_target_pairs={{0,12},{4,8},{8,4},{12,0},{16,28},{20,24},{24,20},{28,16},{32,44},... | collective-permute-start | bytes 1327112 | tf_op jit(solution)/shard_map/ppermute | solution.py:73
  170.0 41.6 %collective-permute-start.18 = (bf16[4,2,2,48,384]{4,3,2,1,0:T(8,128)(2,1)}, bf16[4,2,2,48,384]{4,3,2,1,0:T(8,128)(2,1)}, u32[]{:S(2)}, u32[]{:S(2)}) collective-permute-start(bf16[4,2,2,48,384]{4,3,2,1,0:T(8,128)(2,1)} %pad_maximum_fusion.12), channel_id=1, source_target_pairs={{0,12},{4,8},{8,4},{12,0},{16,28},{20,24},{24,20},{28,16},{32,44},... | collective-permute-start | bytes 1769480 | tf_op jit(solution)/shard_map/ppermute | solution.py:73
  256.7 39.7 %collective-permute-start.42 = (bf16[16,48,1152]{2,1,0:T(8,128)(2,1)}, bf16[16,48,1152]{2,1,0:T(8,128)(2,1)}, u32[]{:S(2)}, u32[]{:S(2)}) collective-permute-start(bf16[16,48,1152]{2,1,0:T(8,128)(2,1)} %constant_dynamic-update-slice_fusion.18.refs_6_), channel_id=1, source_target_pairs={{0,32},{4,36},{8,40},{12,44},{16,48},{20,52},{24,56},{28,60},{32,0... | collective-permute-start | bytes 5308424 | tf_op jit(solution)/shard_map/ppermute | solution.py:73
  260.4 39.4 %collective-permute-start.37 = (bf16[16,48,1152]{2,1,0:T(8,128)(2,1)}, bf16[16,48,1152]{2,1,0:T(8,128)(2,1)}, u32[]{:S(2)}, u32[]{:S(2)}) collective-permute-start(bf16[16,48,1152]{2,1,0:T(8,128)(2,1)} %constant_dynamic-update-slice_fusion.13.refs_4_), channel_id=1, source_target_pairs={{0,4},{4,0},{8,12},{12,8},{16,20},{20,16},{24,28},{28,24},{32,36},... | collective-permute-start | bytes 5308424 | tf_op jit(solution)/shard_map/ppermute | solution.py:73
  268.6 38.7 %collective-permute-start.32 = (bf16[16,48,1152]{2,1,0:T(8,128)(2,1)}, bf16[16,48,1152]{2,1,0:T(8,128)(2,1)}, u32[]{:S(2)}, u32[]{:S(2)}) collective-permute-start(bf16[16,48,1152]{2,1,0:T(8,128)(2,1)} %constant_dynamic-update-slice_fusion.8.refs_2_), channel_id=1, source_target_pairs={{0,16},{4,20},{8,24},{12,28},{16,0},{20,4},{24,8},{28,12},{32,48},... | collective-permute-start | bytes 5308424 | tf_op jit(solution)/shard_map/ppermute | solution.py:73
  270.7 51.0 %collective-permute-start.27 = (bf16[16,48,1152]{2,1,0:T(8,128)(2,1)}, bf16[16,48,1152]{2,1,0:T(8,128)(2,1)}, u32[]{:S(2)}, u32[]{:S(2)}) collective-permute-start(bf16[16,48,1152]{2,1,0:T(8,128)(2,1)} %constant_dynamic-update-slice_fusion.3.refs_0_), channel_id=1, source_target_pairs={{0,96},{4,100},{8,104},{12,108},{16,112},{20,116},{24,120},{28,124... | collective-permute-start | bytes 5308424 | tf_op jit(solution)/shard_map/ppermute | solution.py:73
  376.4 107.0 %collective-permute-start.74 = (bf16[16,48,1152]{2,1,0:T(8,128)(2,1)}, bf16[16,48,1152]{2,1,0:T(8,128)(2,1)}, u32[]{:S(2)}, u32[]{:S(2)}) collective-permute-start(bf16[16,48,1152]{2,1,0:T(8,128)(2,1)} %get-tuple-element.47), channel_id=1, source_target_pairs={{0,32},{4,36},{8,40},{12,44},{16,48},{20,52},{24,56},{28,60},{32,0... | collective-permute-start | bytes 5308424 | tf_op jit(solution)/shard_map/ppermute | solution.py:73
  397.2 90.9 %collective-permute-start.69 = (bf16[16,48,1152]{2,1,0:T(8,128)(2,1)}, bf16[16,48,1152]{2,1,0:T(8,128)(2,1)}, u32[]{:S(2)}, u32[]{:S(2)}) collective-permute-start(bf16[16,48,1152]{2,1,0:T(8,128)(2,1)} %get-tuple-element.45), channel_id=1, source_target_pairs={{0,4},{4,0},{8,12},{12,8},{16,20},{20,16},{24,28},{28,24},{32,36},... | collective-permute-start | bytes 5308424 | tf_op jit(solution)/shard_map/ppermute | solution.py:73
  431.5 64.2 %collective-permute-start.59 = (bf16[16,48,1152]{2,1,0:T(8,128)(2,1)}, bf16[16,48,1152]{2,1,0:T(8,128)(2,1)}, u32[]{:S(2)}, u32[]{:S(2)}) collective-permute-start(bf16[16,48,1152]{2,1,0:T(8,128)(2,1)} %get-tuple-element.41), channel_id=1, source_target_pairs={{0,96},{4,100},{8,104},{12,108},{16,112},{20,116},{24,120},{28,124... | collective-permute-start | bytes 5308424 | tf_op jit(solution)/shard_map/ppermute | solution.py:73
  432.2 65.6 %collective-permute-start.64 = (bf16[16,48,1152]{2,1,0:T(8,128)(2,1)}, bf16[16,48,1152]{2,1,0:T(8,128)(2,1)}, u32[]{:S(2)}, u32[]{:S(2)}) collective-permute-start(bf16[16,48,1152]{2,1,0:T(8,128)(2,1)} %get-tuple-element.43), channel_id=1, source_target_pairs={{0,16},{4,20},{8,24},{12,28},{16,0},{20,4},{24,8},{28,12},{32,48},... | collective-permute-start | bytes 5308424 | tf_op jit(solution)/shard_map/ppermute | solution.py:73
  476.0 39.7 %all-to-all-start.2 = ((bf16[32,256,128]{2,1,0:T(8,128)(2,1)}), bf16[32,256,128]{2,1,0:T(8,128)(2,1)}, u32[]{:S(2)}, u32[]{:S(2)}) async-start(bf16[32,256,128]{2,1,0:T(8,128)(2,1)} %get-tuple-element.37), calls=%async_computation.2 | async-start | bytes 4194304 | tf_op jit(solution)/shard_map/all_to_all | solution.py:911
  548.9 75.2 %all-to-all-start.3 = ((bf16[32,48,1152]{2,1,0:T(8,128)(2,1)}), bf16[32,48,1152]{2,1,0:T(8,128)(2,1)S(1)}, u32[]{:S(2)}, u32[]{:S(2)}) async-start(bf16[32,48,1152]{2,1,0:T(8,128)(2,1)} %bitcast.322), calls=%async_computation.3 | async-start | bytes 7077888 | tf_op jit(solution)/shard_map/all_to_all | solution.py:46
  560.1 52.8 %collective-permute-start.55 = (bf16[2,128,1536]{2,1,0:T(8,128)(2,1)S(1)}, bf16[2,128,1536]{2,1,0:T(8,128)(2,1)S(1)}, u32[]{:S(2)}, u32[]{:S(2)}) collective-permute-start(bf16[2,128,1536]{2,1,0:T(8,128)(2,1)S(1)} %slice.910), channel_id=1, source_target_pairs={{0,1},{1,0},{2,3},{3,2},{4,5},{5,4},{6,7},{7,6},{8,9},{9,8},{10,11... | collective-permute-start | bytes 2359304 | tf_op jit(solution)/shard_map/ppermute | solution.py:144
  562.3 37.3 %collective-permute-start.77 = (bf16[2,48,1152]{2,1,0:T(8,128)(2,1)S(1)}, bf16[2,48,1152]{2,1,0:T(8,128)(2,1)S(1)}, u32[]{:S(2)}, u32[]{:S(2)}) collective-permute-start(bf16[2,48,1152]{2,1,0:T(8,128)(2,1)S(1)} %slice.777), channel_id=1, source_target_pairs={{0,96},{4,100},{8,104},{12,108},{16,112},{20,116},{24,120},{28,124... | collective-permute-start | bytes 663560 | tf_op jit(solution)/shard_map/ppermute | solution.py:73
  566.3 34.1 %collective-permute-start.72 = (bf16[2,48,1152]{2,1,0:T(8,128)(2,1)S(1)}, bf16[2,48,1152]{2,1,0:T(8,128)(2,1)S(1)}, u32[]{:S(2)}, u32[]{:S(2)}) collective-permute-start(bf16[2,48,1152]{2,1,0:T(8,128)(2,1)S(1)} %slice.768), channel_id=1, source_target_pairs={{0,12},{4,8},{8,4},{12,0},{16,28},{20,24},{24,20},{28,16},{32,44},... | collective-permute-start | bytes 663560 | tf_op jit(solution)/shard_map/ppermute | solution.py:73
  568.1 34.9 %collective-permute-start.62 = (bf16[2,48,1152]{2,1,0:T(8,128)(2,1)S(1)}, bf16[2,48,1152]{2,1,0:T(8,128)(2,1)S(1)}, u32[]{:S(2)}, u32[]{:S(2)}) collective-permute-start(bf16[2,48,1152]{2,1,0:T(8,128)(2,1)S(1)} %slice.750), channel_id=1, source_target_pairs={{0,4},{4,0},{8,12},{12,8},{16,20},{20,16},{24,28},{28,24},{32,36},... | collective-permute-start | bytes 663560 | tf_op jit(solution)/shard_map/ppermute | solution.py:73
  570.2 36.9 %collective-permute-start.67 = (bf16[2,48,1152]{2,1,0:T(8,128)(2,1)S(1)}, bf16[2,48,1152]{2,1,0:T(8,128)(2,1)S(1)}, u32[]{:S(2)}, u32[]{:S(2)}) collective-permute-start(bf16[2,48,1152]{2,1,0:T(8,128)(2,1)S(1)} %slice.759), channel_id=1, source_target_pairs={{0,32},{4,36},{8,40},{12,44},{16,48},{20,52},{24,56},{28,60},{32,0... | collective-permute-start | bytes 663560 | tf_op jit(solution)/shard_map/ppermute | solution.py:73
  (219 other events, 2718.5 us)

commit v3 on v2

--- a/solution.py
+++ b/solution.py
@@ -629,7 +629,7 @@
         ],
         compiler_params=pltpu.CompilerParams(vmem_limit_bytes=32 * 1024 * 1024),
         cost_estimate=pl.CostEstimate(
-            flops=steps * 8 * BLOCK * LANES * HEAD_DIM,
+            flops=steps * 42 * BLOCK * LANES * HEAD_DIM,
             bytes_accessed=4 * 1024 * 1024,
             transcendentals=steps * BLOCK * LANES,
         ),

time: 646 us -> 646 us (level)
  no operation moved by 1% of the time
where the time goes in v3:
time: 646 us; the launch traced here: 635 us
  waiting for transfers between devices  163 us (25%)
  starting transfers between devices  144 us (22%)
  Pallas kernels  120 us (19%)
  local copies, waits for them, and re-layouts  96.3 us (15%)
  other arithmetic  79.1 us (12%)
  between operations  19.9 us (3%)
  matrix products  12.4 us (2%)
    ppermute x45, waiting for transfers between devices, across_link(): return lax.ppermute(value, 'ctx', [(i, partner(i)) for i in range(size)])  83.9 us
    ppermute x45, starting transfers between devices, across_link(): return lax.ppermute(value, 'ctx', [(i, partner(i)) for i in range(size)])  62.2 us
    ppermute x22, waiting for transfers between devices, across_ep(): return lax.ppermute(value, 'ep', [(i, i ^ distance) for i in range(4)])  40.4 us
    pallas_call x1, Pallas kernels, attend_back(): pl.pallas_call(backward_kernel, out_shape=(jax.ShapeDtypeStruct(HEADS_SHA...  39.2 us
    unnamed x352, local copies, waits for them, and re-layouts  33.1 us
    ppermute x12, starting transfers between devices, across_quad(): lax.ppermute(value, 'ctx', [(i, quad_member(i, size, distance)) for i in...  31.6 us
    pallas_call x1, Pallas kernels, attend(): pl.pallas_call(forward_kernel, out_shape=(jax.ShapeDtypeStruct(HEADS_SHAP...  31 us
    pallas_call x1, Pallas kernels, run_experts(): pl.pallas_call(experts_kernel, out_shape=(jax.ShapeDtypeStruct((*kept_row...  27.4 us
  transfers between devices with their start and end apart: 83, of which 20 were waited for; matrix products, arithmetic and copies ran while one was open for 26% of the time, Pallas kernels for 15%

profile of v3, /device:TPU:26, one launch (start us, length us, event | category | flops | bytes accessed | tf_op | source)
XLA Modules:
  0.0 634.7 jit_solution(8138971261668422147)
XLA Ops:
  34.4 9.4 %all-to-all-start = ((bf16[32,48,768]{2,1,0:T(8,128)(2,1)}), bf16[32,48,768]{2,1,0:T(8,128)(2,1)}, u32[]{:S(2)}, u32[]{:S(2)}) async-start(bf16[32,48,768]{2,1,0:T(8,128)(2,1)} %broadcast_in_dim.26), calls=%async_computation | async-start | bytes 4718592 | tf_op jit(solution)/shard_map/all_to_all | solution.py:42
  52.7 22.8 %all-to-all-done = bf16[32,48,768]{2,1,0:T(8,128)(2,1)} async-done(((bf16[32,48,768]{2,1,0:T(8,128)(2,1)}), bf16[32,48,768]{2,1,0:T(8,128)(2,1)}, u32[]{:S(2)}, u32[]{:S(2)}) %all-to-all-start) | async-done | bytes 2359328 | tf_op jit(solution)/shard_map/all_to_all | solution.py:42
  96.5 7.2 %all-to-all-start.1 = ((bf16[32,256,128]{2,1,0:T(8,128)(2,1)}), bf16[32,256,128]{2,1,0:T(8,128)(2,1)S(1)}, u32[]{:S(2)}, u32[]{:S(2)}) async-start(bf16[32,256,128]{2,1,0:T(8,128)(2,1)} %bitcast.323), calls=%async_computation.1 | async-start | bytes 4194304 | tf_op jit(solution)/shard_map/all_to_all | solution.py:816
  177.9 31.0 %attend.1 = (f32[4,3,64,256]{3,2,1,0:T(8,128)S(1)}, f32[4,1,768]{2,1,0:T(1,128)S(1)}) custom-call(s32[4]{0:T(128)S(1)} %add_add_fusion.2.blocks_ref, bf16[4,3,64,256]{3,2,1,0:T(8,128)(2,1)S(1)} %pad_maximum_fusion.17.q_ref, bf16[32,256,128]{2,1,0:T(8,128)(2,1)S(1)} %all-to-all-done.1.kv_ref, f32[4,1,768]{2,1,0:T(1,128)S(1)} %copy.289.seg_row_ref, ...), custom_call_target="tpu_custom_call" | custom-call | flops 34879832064 | bytes 4194304 | tf_op jit(solution)/shard_map/attend/pallas_call | solution.py:616
  211.6 5.4 collective-permute-start.13
  241.1 15.6 %collective-permute-done.20 = bf16[2,64,1536]{2,1,0:T(8,128)(2,1)S(1)} collective-permute-done((bf16[2,64,1536]{2,1,0:T(8,128)(2,1)S(1)}, bf16[2,64,1536]{2,1,0:T(8,128)(2,1)S(1)}, u32[]{:S(2)}, u32[]{:S(2)}) %collective-permute-start.20) | collective-permute-done | bytes 393248 | tf_op jit(solution)/shard_map/ppermute | solution.py:144
  262.5 6.2 collective-permute-done.21
  270.7 11.0 %collective-permute-start.27 = (bf16[16,48,1152]{2,1,0:T(8,128)(2,1)}, bf16[16,48,1152]{2,1,0:T(8,128)(2,1)}, u32[]{:S(2)}, u32[]{:S(2)}) collective-permute-start(bf16[16,48,1152]{2,1,0:T(8,128)(2,1)} %constant_dynamic-update-slice_fusion.3.refs_0_), channel_id=1, source_target_pairs={{0,96},{4,100},{8,104},{12,108},{16,112},{20,116},{24,120},{28,124... | collective-permute-start | bytes 5308424 | tf_op jit(solution)/shard_map/ppermute | solution.py:73
  284.3 12.0 %collective-permute-done.42.refs_7_ = bf16[16,48,1152]{2,1,0:T(8,128)(2,1)} collective-permute-done((bf16[16,48,1152]{2,1,0:T(8,128)(2,1)}, bf16[16,48,1152]{2,1,0:T(8,128)(2,1)}, u32[]{:S(2)}, u32[]{:S(2)}) %collective-permute-start.42) | collective-permute-done | bytes 1769504 | tf_op jit(solution)/shard_map/ppermute | solution.py:73
  299.8 7.6 %collective-permute-done.32.refs_3_ = bf16[16,48,1152]{2,1,0:T(8,128)(2,1)} collective-permute-done((bf16[16,48,1152]{2,1,0:T(8,128)(2,1)}, bf16[16,48,1152]{2,1,0:T(8,128)(2,1)}, u32[]{:S(2)}, u32[]{:S(2)}) %collective-permute-start.32) | collective-permute-done | bytes 1769504 | tf_op jit(solution)/shard_map/ppermute | solution.py:73
  307.4 14.4 %collective-permute-done.27.refs_1_ = bf16[16,48,1152]{2,1,0:T(8,128)(2,1)} collective-permute-done((bf16[16,48,1152]{2,1,0:T(8,128)(2,1)}, bf16[16,48,1152]{2,1,0:T(8,128)(2,1)}, u32[]{:S(2)}, u32[]{:S(2)}) %collective-permute-start.27) | collective-permute-done | bytes 1769504 | tf_op jit(solution)/shard_map/ppermute | solution.py:73
  321.8 27.4 %run_experts.1 = (f32[2,128,1664]{2,1,0:T(8,128)}, bf16[2,128,1664]{2,1,0:T(8,128)(2,1)}, f32[2,128,1536]{2,1,0:T(8,128)S(1)}, bf16[2,128,1536]{2,1,0:T(8,128)(2...) custom-call(s32[4,32]{1,0:T(4,128)S(1)} %broadcast_xor_fusion.places_ref, s32[1]{0:T(128)} %bitcast.55.ep_ref, ...), custom_call_target="tpu_custom_call" | custom-call | flops 14495514624 | bytes 31457280 | tf_op jit(solution)/shard_map/run_experts/pallas_call | solution.py:557
  370.8 5.5 expert_grads.7
  377.2 7.9 %collective-permute-done.46 = bf16[2,64,1664]{2,1,0:T(8,128)(2,1)S(1)} collective-permute-done((bf16[2,64,1664]{2,1,0:T(8,128)(2,1)S(1)}, bf16[2,64,1664]{2,1,0:T(8,128)(2,1)S(1)}, u32[]{:S(2)}, u32[]{:S(2)}) %collective-permute-start.46) | collective-permute-done | bytes 426016 | tf_op jit(solution)/shard_map/ppermute | solution.py:144
  390.1 6.0 expert_grads.6
  398.9 5.6 expert_grads.4
  405.7 5.5 expert_grads.5
  436.8 39.2 %attend_back.1 = (bf16[4,3,64,256]{3,2,1,0:T(8,128)(2,1)S(1)}, bf16[32,256,128]{2,1,0:T(8,128)(2,1)}) custom-call(s32[4]{0:T(128)S(1)} %add_add_fusion.1.blocks_ref, bf16[4,3,64,256]{3,2,1,0:T(8,128)(2,1)S(1)} %pad_maximum_fusion.17.q_ref, bf16[4,3,64,256]{3,2,1,0:T(8,128)(2,1)S(1)} %pad_maximum_fusion.20.do_ref, bf16[32,256,128]{2,1,0:T(8,128)(2,1)S(1)} %copy-done.7, ...), custom_call_target="tpu_custom_call" | custom-call | flops 16609443840 | bytes 6291456 | tf_op jit(solution)/shard_map/attend_back/pallas_call | solution.py:642
  476.0 5.8 all-to-all-start.2
  502.6 8.5 %collective-permute-done.52 = bf16[3,64,256]{2,1,0:T(8,128)(2,1)S(1)} collective-permute-done((bf16[3,64,256]{2,1,0:T(8,128)(2,1)S(1)}, bf16[3,64,256]{2,1,0:T(8,128)(2,1)S(1)}, u32[]{:S(2)}, u32[]{:S(2)}) %collective-permute-start.52) | collective-permute-done | bytes 98336 | tf_op jit(solution)/shard_map/ppermute | solution.py:185
  517.6 7.5 %collective-permute-done.75 = bf16[8,48,1152]{2,1,0:T(8,128)(2,1)} collective-permute-done((bf16[8,48,1152]{2,1,0:T(8,128)(2,1)}, bf16[8,48,1152]{2,1,0:T(8,128)(2,1)}, u32[]{:S(2)}, u32[]{:S(2)}) %collective-permute-start.75) | collective-permute-done | bytes 884768 | tf_op jit(solution)/shard_map/ppermute | solution.py:73
  548.9 7.2 %all-to-all-start.3 = ((bf16[32,48,1152]{2,1,0:T(8,128)(2,1)}), bf16[32,48,1152]{2,1,0:T(8,128)(2,1)S(1)}, u32[]{:S(2)}, u32[]{:S(2)}) async-start(bf16[32,48,1152]{2,1,0:T(8,128)(2,1)} %bitcast.322), calls=%async_computation.3 | async-start | bytes 7077888 | tf_op jit(solution)/shard_map/all_to_all | solution.py:46
  570.5 29.2 %collective-permute-done.77 = bf16[2,48,1152]{2,1,0:T(8,128)(2,1)S(1)} collective-permute-done((bf16[2,48,1152]{2,1,0:T(8,128)(2,1)S(1)}, bf16[2,48,1152]{2,1,0:T(8,128)(2,1)S(1)}, u32[]{:S(2)}, u32[]{:S(2)}) %collective-permute-start.77) | collective-permute-done | bytes 221216 | tf_op jit(solution)/shard_map/ppermute | solution.py:73
  616.3 6.2 collective-permute-done.56
  (776 shorter events, 310.7 us)
Async XLA Ops:
  6.5 38.8 %collective-permute-start = (bf16[2,64,1536]{2,1,0:T(8,128)(2,1)}, bf16[2,64,1536]{2,1,0:T(8,128)(2,1)S(1)}, u32[]{:S(2)}, u32[]{:S(2)}) collective-permute-start(bf16[2,64,1536]{2,1,0:T(8,128)(2,1)} %param.24), channel_id=1, source_target_pairs={{0,2},{1,3},{2,0},{3,1},{4,6},{5,7},{6,4},{7,5},{8,10},{9,11},{10,... | collective-permute-start | bytes 1179656 | tf_op jit(solution)/shard_map/ppermute | solution.py:144
  9.5 37.1 %collective-permute-start.2 = (bf16[2,64,128]{1,0,2:T(2,128)(2,1)S(1)}, bf16[2,64,128]{1,0,2:T(2,128)(2,1)S(1)}, u32[]{:S(2)}, u32[]{:S(2)}) collective-permute-start(bf16[2,64,128]{1,0,2:T(2,128)(2,1)S(1)} %pad_convert_fusion), channel_id=1, source_target_pairs={{0,2},{1,3},{2,0},{3,1},{4,6},{5,7},{6,4},{7,5},{8,10},{9,11},{10,... | collective-permute-start | bytes 98312 | tf_op jit(solution)/shard_map/ppermute | solution.py:144
  34.4 41.2 %all-to-all-start = ((bf16[32,48,768]{2,1,0:T(8,128)(2,1)}), bf16[32,48,768]{2,1,0:T(8,128)(2,1)}, u32[]{:S(2)}, u32[]{:S(2)}) async-start(bf16[32,48,768]{2,1,0:T(8,128)(2,1)} %broadcast_in_dim.26), calls=%async_computation | async-start | bytes 4718592 | tf_op jit(solution)/shard_map/all_to_all | solution.py:42
  47.4 223.3 %collective-permute-start.3 = (bf16[2,128,128]{1,0,2:T(2,128)(2,1)}, bf16[2,128,128]{1,0,2:T(2,128)(2,1)}, u32[]{:S(2)}, u32[]{:S(2)}) collective-permute-start(bf16[2,128,128]{1,0,2:T(2,128)(2,1)} %pad_maximum_fusion.40), channel_id=1, source_target_pairs={{0,1},{1,0},{2,3},{3,2},{4,5},{5,4},{6,7},{7,6},{8,9},{9,8},{10,11... | collective-permute-start | bytes 196616 | tf_op jit(solution)/shard_map/ppermute | solution.py:144
  86.2 52.7 %collective-permute-start.38 = (bf16[1,48,1152]{2,1,0:T(8,128)(2,1)S(1)}, bf16[1,48,1152]{2,1,0:T(8,128)(2,1)S(1)}, u32[]{:S(2)}, u32[]{:S(2)}) collective-permute-start(bf16[1,48,1152]{2,1,0:T(8,128)(2,1)S(1)} %get-tuple-element.67), channel_id=1, source_target_pairs={{0,12},{4,8},{8,4},{12,0},{16,28},{20,24},{24,20},{28,16},{32,44},... | collective-permute-start | bytes 331784 | tf_op jit(solution)/shard_map/ppermute | solution.py:73
  87.4 39.9 %collective-permute-start.14 = (bf16[1,1,1,48,384]{4,3,2,1,0:T(8,128)(2,1)}, bf16[1,1,1,48,384]{4,3,2,1,0:T(8,128)(2,1)}, u32[]{:S(2)}, u32[]{:S(2)}) collective-permute-start(bf16[1,1,1,48,384]{4,3,2,1,0:T(8,128)(2,1)} %get-tuple-element.167), channel_id=1, source_target_pairs={{0,96},{4,100},{8,104},{12,108},{16,112},{20,116},{24,120},{28,124... | collective-permute-start | bytes 110600 | tf_op jit(solution)/shard_map/ppermute | solution.py:73
  96.5 80.4 %all-to-all-start.1 = ((bf16[32,256,128]{2,1,0:T(8,128)(2,1)}), bf16[32,256,128]{2,1,0:T(8,128)(2,1)S(1)}, u32[]{:S(2)}, u32[]{:S(2)}) async-start(bf16[32,256,128]{2,1,0:T(8,128)(2,1)} %bitcast.323), calls=%async_computation.1 | async-start | bytes 4194304 | tf_op jit(solution)/shard_map/all_to_all | solution.py:816
  164.9 60.9 %collective-permute-start.30 = (bf16[4,48,1152]{2,1,0:T(8,128)(2,1)}, bf16[4,48,1152]{2,1,0:T(8,128)(2,1)}, u32[]{:S(2)}, u32[]{:S(2)}) collective-permute-start(bf16[4,48,1152]{2,1,0:T(8,128)(2,1)} %pad_maximum_fusion.14), channel_id=1, source_target_pairs={{0,12},{4,8},{8,4},{12,0},{16,28},{20,24},{24,20},{28,16},{32,44},... | collective-permute-start | bytes 1327112 | tf_op jit(solution)/shard_map/ppermute | solution.py:73
  170.0 41.6 %collective-permute-start.18 = (bf16[4,2,2,48,384]{4,3,2,1,0:T(8,128)(2,1)}, bf16[4,2,2,48,384]{4,3,2,1,0:T(8,128)(2,1)}, u32[]{:S(2)}, u32[]{:S(2)}) collective-permute-start(bf16[4,2,2,48,384]{4,3,2,1,0:T(8,128)(2,1)} %pad_maximum_fusion.12), channel_id=1, source_target_pairs={{0,12},{4,8},{8,4},{12,0},{16,28},{20,24},{24,20},{28,16},{32,44},... | collective-permute-start | bytes 1769480 | tf_op jit(solution)/shard_map/ppermute | solution.py:73
  256.7 39.7 %collective-permute-start.42 = (bf16[16,48,1152]{2,1,0:T(8,128)(2,1)}, bf16[16,48,1152]{2,1,0:T(8,128)(2,1)}, u32[]{:S(2)}, u32[]{:S(2)}) collective-permute-start(bf16[16,48,1152]{2,1,0:T(8,128)(2,1)} %constant_dynamic-update-slice_fusion.18.refs_6_), channel_id=1, source_target_pairs={{0,32},{4,36},{8,40},{12,44},{16,48},{20,52},{24,56},{28,60},{32,0... | collective-permute-start | bytes 5308424 | tf_op jit(solution)/shard_map/ppermute | solution.py:73
  260.4 39.4 %collective-permute-start.37 = (bf16[16,48,1152]{2,1,0:T(8,128)(2,1)}, bf16[16,48,1152]{2,1,0:T(8,128)(2,1)}, u32[]{:S(2)}, u32[]{:S(2)}) collective-permute-start(bf16[16,48,1152]{2,1,0:T(8,128)(2,1)} %constant_dynamic-update-slice_fusion.13.refs_4_), channel_id=1, source_target_pairs={{0,4},{4,0},{8,12},{12,8},{16,20},{20,16},{24,28},{28,24},{32,36},... | collective-permute-start | bytes 5308424 | tf_op jit(solution)/shard_map/ppermute | solution.py:73
  268.6 38.7 %collective-permute-start.32 = (bf16[16,48,1152]{2,1,0:T(8,128)(2,1)}, bf16[16,48,1152]{2,1,0:T(8,128)(2,1)}, u32[]{:S(2)}, u32[]{:S(2)}) collective-permute-start(bf16[16,48,1152]{2,1,0:T(8,128)(2,1)} %constant_dynamic-update-slice_fusion.8.refs_2_), channel_id=1, source_target_pairs={{0,16},{4,20},{8,24},{12,28},{16,0},{20,4},{24,8},{28,12},{32,48},... | collective-permute-start | bytes 5308424 | tf_op jit(solution)/shard_map/ppermute | solution.py:73
  270.7 51.0 %collective-permute-start.27 = (bf16[16,48,1152]{2,1,0:T(8,128)(2,1)}, bf16[16,48,1152]{2,1,0:T(8,128)(2,1)}, u32[]{:S(2)}, u32[]{:S(2)}) collective-permute-start(bf16[16,48,1152]{2,1,0:T(8,128)(2,1)} %constant_dynamic-update-slice_fusion.3.refs_0_), channel_id=1, source_target_pairs={{0,96},{4,100},{8,104},{12,108},{16,112},{20,116},{24,120},{28,124... | collective-permute-start | bytes 5308424 | tf_op jit(solution)/shard_map/ppermute | solution.py:73
  376.4 107.0 %collective-permute-start.74 = (bf16[16,48,1152]{2,1,0:T(8,128)(2,1)}, bf16[16,48,1152]{2,1,0:T(8,128)(2,1)}, u32[]{:S(2)}, u32[]{:S(2)}) collective-permute-start(bf16[16,48,1152]{2,1,0:T(8,128)(2,1)} %get-tuple-element.47), channel_id=1, source_target_pairs={{0,32},{4,36},{8,40},{12,44},{16,48},{20,52},{24,56},{28,60},{32,0... | collective-permute-start | bytes 5308424 | tf_op jit(solution)/shard_map/ppermute | solution.py:73
  397.2 90.9 %collective-permute-start.69 = (bf16[16,48,1152]{2,1,0:T(8,128)(2,1)}, bf16[16,48,1152]{2,1,0:T(8,128)(2,1)}, u32[]{:S(2)}, u32[]{:S(2)}) collective-permute-start(bf16[16,48,1152]{2,1,0:T(8,128)(2,1)} %get-tuple-element.45), channel_id=1, source_target_pairs={{0,4},{4,0},{8,12},{12,8},{16,20},{20,16},{24,28},{28,24},{32,36},... | collective-permute-start | bytes 5308424 | tf_op jit(solution)/shard_map/ppermute | solution.py:73
  431.5 64.2 %collective-permute-start.59 = (bf16[16,48,1152]{2,1,0:T(8,128)(2,1)}, bf16[16,48,1152]{2,1,0:T(8,128)(2,1)}, u32[]{:S(2)}, u32[]{:S(2)}) collective-permute-start(bf16[16,48,1152]{2,1,0:T(8,128)(2,1)} %get-tuple-element.41), channel_id=1, source_target_pairs={{0,96},{4,100},{8,104},{12,108},{16,112},{20,116},{24,120},{28,124... | collective-permute-start | bytes 5308424 | tf_op jit(solution)/shard_map/ppermute | solution.py:73
  432.2 65.6 %collective-permute-start.64 = (bf16[16,48,1152]{2,1,0:T(8,128)(2,1)}, bf16[16,48,1152]{2,1,0:T(8,128)(2,1)}, u32[]{:S(2)}, u32[]{:S(2)}) collective-permute-start(bf16[16,48,1152]{2,1,0:T(8,128)(2,1)} %get-tuple-element.43), channel_id=1, source_target_pairs={{0,16},{4,20},{8,24},{12,28},{16,0},{20,4},{24,8},{28,12},{32,48},... | collective-permute-start | bytes 5308424 | tf_op jit(solution)/shard_map/ppermute | solution.py:73
  476.0 39.7 %all-to-all-start.2 = ((bf16[32,256,128]{2,1,0:T(8,128)(2,1)}), bf16[32,256,128]{2,1,0:T(8,128)(2,1)}, u32[]{:S(2)}, u32[]{:S(2)}) async-start(bf16[32,256,128]{2,1,0:T(8,128)(2,1)} %get-tuple-element.37), calls=%async_computation.2 | async-start | bytes 4194304 | tf_op jit(solution)/shard_map/all_to_all | solution.py:911
  548.9 75.2 %all-to-all-start.3 = ((bf16[32,48,1152]{2,1,0:T(8,128)(2,1)}), bf16[32,48,1152]{2,1,0:T(8,128)(2,1)S(1)}, u32[]{:S(2)}, u32[]{:S(2)}) async-start(bf16[32,48,1152]{2,1,0:T(8,128)(2,1)} %bitcast.322), calls=%async_computation.3 | async-start | bytes 7077888 | tf_op jit(solution)/shard_map/all_to_all | solution.py:46
  560.1 52.8 %collective-permute-start.55 = (bf16[2,128,1536]{2,1,0:T(8,128)(2,1)S(1)}, bf16[2,128,1536]{2,1,0:T(8,128)(2,1)S(1)}, u32[]{:S(2)}, u32[]{:S(2)}) collective-permute-start(bf16[2,128,1536]{2,1,0:T(8,128)(2,1)S(1)} %slice.910), channel_id=1, source_target_pairs={{0,1},{1,0},{2,3},{3,2},{4,5},{5,4},{6,7},{7,6},{8,9},{9,8},{10,11... | collective-permute-start | bytes 2359304 | tf_op jit(solution)/shard_map/ppermute | solution.py:144
  562.3 37.3 %collective-permute-start.77 = (bf16[2,48,1152]{2,1,0:T(8,128)(2,1)S(1)}, bf16[2,48,1152]{2,1,0:T(8,128)(2,1)S(1)}, u32[]{:S(2)}, u32[]{:S(2)}) collective-permute-start(bf16[2,48,1152]{2,1,0:T(8,128)(2,1)S(1)} %slice.777), channel_id=1, source_target_pairs={{0,96},{4,100},{8,104},{12,108},{16,112},{20,116},{24,120},{28,124... | collective-permute-start | bytes 663560 | tf_op jit(solution)/shard_map/ppermute | solution.py:73
  566.3 34.1 %collective-permute-start.72 = (bf16[2,48,1152]{2,1,0:T(8,128)(2,1)S(1)}, bf16[2,48,1152]{2,1,0:T(8,128)(2,1)S(1)}, u32[]{:S(2)}, u32[]{:S(2)}) collective-permute-start(bf16[2,48,1152]{2,1,0:T(8,128)(2,1)S(1)} %slice.768), channel_id=1, source_target_pairs={{0,12},{4,8},{8,4},{12,0},{16,28},{20,24},{24,20},{28,16},{32,44},... | collective-permute-start | bytes 663560 | tf_op jit(solution)/shard_map/ppermute | solution.py:73
  568.1 34.9 %collective-permute-start.62 = (bf16[2,48,1152]{2,1,0:T(8,128)(2,1)S(1)}, bf16[2,48,1152]{2,1,0:T(8,128)(2,1)S(1)}, u32[]{:S(2)}, u32[]{:S(2)}) collective-permute-start(bf16[2,48,1152]{2,1,0:T(8,128)(2,1)S(1)} %slice.750), channel_id=1, source_target_pairs={{0,4},{4,0},{8,12},{12,8},{16,20},{20,16},{24,28},{28,24},{32,36},... | collective-permute-start | bytes 663560 | tf_op jit(solution)/shard_map/ppermute | solution.py:73
  570.2 36.9 %collective-permute-start.67 = (bf16[2,48,1152]{2,1,0:T(8,128)(2,1)S(1)}, bf16[2,48,1152]{2,1,0:T(8,128)(2,1)S(1)}, u32[]{:S(2)}, u32[]{:S(2)}) collective-permute-start(bf16[2,48,1152]{2,1,0:T(8,128)(2,1)S(1)} %slice.759), channel_id=1, source_target_pairs={{0,32},{4,36},{8,40},{12,44},{16,48},{20,52},{24,56},{28,60},{32,0... | collective-permute-start | bytes 663560 | tf_op jit(solution)/shard_map/ppermute | solution.py:73
  (219 other events, 2718.5 us)
